TPU v7x, 512 devices: a whole 4x8x8 slice. The times are simulated.
512 devices in a mesh: row: 64 (over x, z, y_hi), col: 8 (over y_lo, core).
Axes of the slice: x: 4, y: 8 (y_hi: 2, y_lo: 4; y = y_hi * 4 + y_lo), z: 8, core: 2. Of those that a mesh axis runs over, the one named last changes fastest.
Arguments:
- matrix: float32 [65536, 2048], P('row', 'col'), may hold values from -6 to 6
- signs: int32 [65536], P('row'), may hold values from -1 to 1, as said below
- picks: int32 [16384], P('row'), may hold values from 0 to 65535, as said below
Outputs:
- sketch: float32 [16384, 2048], P('row', 'col')
- gram: float32 [2048, 2048], P('row', 'col')
Inputs may be any that keep to these rules, and one draw needn't show every extreme that they name: `signs`: each entry is +1 or -1. `picks`: sorted and distinct; entries k * 256 to (k + 1) * 256 - 1 lie in rows k * 1024 to (k + 1) * 1024 - 1.
All inputs are finite; a program needn't handle non-finite values.
Results may differ from a plain program's by a relative error of at most 0.00013.
Values sent between devices are 32-bit elements; how exact they have to be, the bound alone decides.
No kernel may reach another device: no remote copies, remote signals or barrier semaphores. Data moves between devices by JAX's collectives and lax.ppermute only.
A program may use at most 64 MiB of HBM per device.

v0:
```python
import jax
import jax.numpy as jnp
from jax import lax
from jax.sharding import PartitionSpec as P


def from_partner(x, axis, distance):
    return lax.ppermute(x, axis, [(i, i ^ 1 << distance) for i in range(lax.axis_size(axis))])


def sylvester(order):
    left = lax.broadcasted_iota(jnp.int32, (order, order), 0)
    right = lax.broadcasted_iota(jnp.int32, (order, order), 1)
    both = jnp.bitwise_and(left, right)
    parity = jnp.zeros((order, order), jnp.int32)
    for shift_bit in range(order.bit_length() - 1):
        parity = jnp.bitwise_xor(parity, jnp.bitwise_and(jnp.right_shift(both, shift_bit), 1))
    return (1 - 2 * parity).astype(jnp.float32)


def shards(matrix, signs, picks):
    local_rows = matrix.shape[0]
    groups = lax.axis_size("row")
    position = lax.axis_index("row")
    offsets = picks - position * local_rows
    scale = jnp.float32(1.0 / (local_rows * groups) ** 0.5)
    signed = matrix * signs.astype(jnp.float32)[:, None]
    local_table = sylvester(local_rows)
    mixed = jnp.dot(
        local_table, signed, precision=lax.Precision.HIGHEST, preferred_element_type=jnp.float32
    )
    for section_bit in range(groups.bit_length() - 1):
        partner = from_partner(mixed, "row", section_bit)
        upper = jnp.bitwise_and(jnp.right_shift(position, section_bit), 1) == 1
        mixed = jnp.where(upper, partner - mixed, mixed + partner)
    sketch = jnp.take(mixed * scale, offsets, axis=0)
    full_rows = lax.all_gather(sketch, "col", axis=1, tiled=True)
    total_samples = sketch.shape[0] * groups
    gram = lax.psum_scatter(
        jnp.dot(
            full_rows.T, sketch, precision=lax.Precision.HIGHEST, preferred_element_type=jnp.float32
        ),
        "row",
        scatter_dimension=0,
        tiled=True,
    )
    return (sketch, gram / jnp.float32(total_samples))


def solution(mesh):
    placed = (P("row", "col"), P("row"), P("row"))
    return jax.shard_map(
        shards,
        mesh=mesh,
        in_specs=placed,
        out_specs=(P("row", "col"), P("row", "col")),
        check_vma=False,
    )
```

profile of v0, /device:TPU:8, one launch (start us, length us, event | category | flops | bytes accessed | tf_op | source)
XLA Modules:
  0.0 761.2 jit_solution(17460994881732774814)
XLA Ops:
  7.2 0.7 convert_element_type.7
  7.9 9.0 %fusion = f32[1024,256]{1,0:T(8,128)S(1)} fusion(f32[1024,256]{1,0:T(8,128)} %param.3, f32[1024]{0:T(1024)S(1)} %convert_element_type.7), kind=kOutput, calls=%fused_computation.1 | convolution fusion | flops 3256090624 | bytes 2101248 | tf_op jit(solution)/shard_map/dot_general | solution.py:29
  16.9 6.8 collective-permute-start
  23.8 46.3 %collective-permute-done = f32[1024,256]{1,0:T(8,128)S(1)} collective-permute-done((f32[1024,256]{1,0:T(8,128)S(1)}, f32[1024,256]{1,0:T(8,128)S(1)}, u32[]{:S(2)}, u32[]{:S(2)}) %collective-permute-start) | collective-permute-done | bytes 1048608 | tf_op jit(solution)/shard_map/ppermute | solution.py:8
  70.2 4.3 collective-permute-start.1
  74.5 22.3 %collective-permute-done.1 = f32[1024,256]{1,0:T(8,128)S(1)} collective-permute-done((f32[1024,256]{1,0:T(8,128)S(1)}, f32[1024,256]{1,0:T(8,128)S(1)}, u32[]{:S(2)}, u32[]{:S(2)}) %collective-permute-start.1) | collective-permute-done | bytes 1048608 | tf_op jit(solution)/shard_map/ppermute | solution.py:8
  96.8 0.1 add_select_fusion.3
  96.9 6.1 collective-permute-start.2
  103.0 44.1 %collective-permute-done.2 = f32[1024,256]{1,0:T(8,128)S(1)} collective-permute-done((f32[1024,256]{1,0:T(8,128)S(1)}, f32[1024,256]{1,0:T(8,128)S(1)}, u32[]{:S(2)}, u32[]{:S(2)}) %collective-permute-start.2) | collective-permute-done | bytes 1048608 | tf_op jit(solution)/shard_map/ppermute | solution.py:8
  147.3 8.4 %collective-permute-start.3 = (f32[1024,256]{1,0:T(8,128)S(1)}, f32[1024,256]{1,0:T(8,128)S(1)}, u32[]{:S(2)}, u32[]{:S(2)}) collective-permute-start(f32[1024,256]{1,0:T(8,128)S(1)} %add_select_fusion.2), channel_id=1, source_target_pairs={{0,64},{8,72},{16,80},{24,88},{32,96},{40,104},{48,112},{56,120},{... | collective-permute-start | bytes 3145736 | tf_op jit(solution)/shard_map/ppermute | solution.py:8
  155.7 45.3 %collective-permute-done.3 = f32[1024,256]{1,0:T(8,128)S(1)} collective-permute-done((f32[1024,256]{1,0:T(8,128)S(1)}, f32[1024,256]{1,0:T(8,128)S(1)}, u32[]{:S(2)}, u32[]{:S(2)}) %collective-permute-start.3) | collective-permute-done | bytes 1048608 | tf_op jit(solution)/shard_map/ppermute | solution.py:8
  201.0 0.1 add_select_fusion.1
  201.1 3.4 collective-permute-start.4
  204.6 21.9 %collective-permute-done.4 = f32[1024,256]{1,0:T(8,128)S(1)} collective-permute-done((f32[1024,256]{1,0:T(8,128)S(1)}, f32[1024,256]{1,0:T(8,128)S(1)}, u32[]{:S(2)}, u32[]{:S(2)}) %collective-permute-start.4) | collective-permute-done | bytes 1048608 | tf_op jit(solution)/shard_map/ppermute | solution.py:8
  226.6 5.0 collective-permute-start.5
  231.6 20.9 %collective-permute-done.5 = f32[1024,256]{1,0:T(8,128)S(1)} collective-permute-done((f32[1024,256]{1,0:T(8,128)S(1)}, f32[1024,256]{1,0:T(8,128)S(1)}, u32[]{:S(2)}, u32[]{:S(2)}) %collective-permute-start.5) | collective-permute-done | bytes 1048608 | tf_op jit(solution)/shard_map/ppermute | solution.py:8
  252.4 0.1 select_multiply_fusion
  252.6 1.0 gather_fusion
  253.6 0.8 broadcast_select_fusion
  254.4 0.2 reduce-scatter.2.cloned.1.call-start
  254.6 40.7 %all-gather.2.cloned.1.call-done = f32[256,2048]{1,0:T(8,128)} async-done(((f32[256,256]{1,0:T(8,128)}), f32[256,2048]{1,0:T(8,128)}) %all-gather.2.cloned.1.call-update) | async-done | bytes 2097168 | tf_op jit(solution)/shard_map/all_gather | solution.py:37
  295.3 6.4 fusion.58
  301.7 451.3 %reduce-scatter.2.cloned.1.call-done = f32[32,256]{1,0:T(8,128)} async-done(((f32[2048,256]{1,0:T(8,128)}), f32[32,256]{1,0:T(8,128)}) %reduce-scatter.2.cloned.1.call-update) | async-done | bytes 32784 | tf_op jit(solution)/shard_map/reduce_scatter | solution.py:39
  753.0 1.4 broadcast_multiply_fusion
  (10 shorter events, 0.5 us)
Async XLA Ops:
  7.2 288.1 %all-gather.2.cloned.1.call-start = ((), (), s32[]{:S(2)}) async-start(), calls=%async_computation.1 | async-start | bytes 2359296 | tf_op jit(solution)/shard_map/all_gather | solution.py:37
  16.9 53.2 %collective-permute-start = (f32[1024,256]{1,0:T(8,128)S(1)}, f32[1024,256]{1,0:T(8,128)S(1)}, u32[]{:S(2)}, u32[]{:S(2)}) collective-permute-start(f32[1024,256]{1,0:T(8,128)S(1)} %fusion), channel_id=1, source_target_pairs={{0,8},{8,0},{16,24},{24,16},{32,40},{40,32},{48,56},{56,48},{64,72... | collective-permute-start | bytes 3145736 | tf_op jit(solution)/shard_map/ppermute | solution.py:8
  70.2 26.6 %collective-permute-start.1 = (f32[1024,256]{1,0:T(8,128)S(1)}, f32[1024,256]{1,0:T(8,128)S(1)}, u32[]{:S(2)}, u32[]{:S(2)}) collective-permute-start(f32[1024,256]{1,0:T(8,128)S(1)} %add_select_fusion.4), channel_id=1, source_target_pairs={{0,16},{8,24},{16,0},{24,8},{32,48},{40,56},{48,32},{56,40},{64,80... | collective-permute-start | bytes 3145736 | tf_op jit(solution)/shard_map/ppermute | solution.py:8
  96.9 50.2 %collective-permute-start.2 = (f32[1024,256]{1,0:T(8,128)S(1)}, f32[1024,256]{1,0:T(8,128)S(1)}, u32[]{:S(2)}, u32[]{:S(2)}) collective-permute-start(f32[1024,256]{1,0:T(8,128)S(1)} %add_select_fusion.3), channel_id=1, source_target_pairs={{0,32},{8,40},{16,48},{24,56},{32,0},{40,8},{48,16},{56,24},{64,96... | collective-permute-start | bytes 3145736 | tf_op jit(solution)/shard_map/ppermute | solution.py:8
  147.3 53.7 %collective-permute-start.3 = (f32[1024,256]{1,0:T(8,128)S(1)}, f32[1024,256]{1,0:T(8,128)S(1)}, u32[]{:S(2)}, u32[]{:S(2)}) collective-permute-start(f32[1024,256]{1,0:T(8,128)S(1)} %add_select_fusion.2), channel_id=1, source_target_pairs={{0,64},{8,72},{16,80},{24,88},{32,96},{40,104},{48,112},{56,120},{... | collective-permute-start | bytes 3145736 | tf_op jit(solution)/shard_map/ppermute | solution.py:8
  201.1 30.4 %copy-start = (s32[256]{0:T(256)S(1)}, s32[256]{0:T(256)}, u32[]{:S(2)}) copy-start(s32[256]{0:T(256)} %param.5) | copy-start | bytes 3076
  201.1 25.3 %collective-permute-start.4 = (f32[1024,256]{1,0:T(8,128)S(1)}, f32[1024,256]{1,0:T(8,128)S(1)}, u32[]{:S(2)}, u32[]{:S(2)}) collective-permute-start(f32[1024,256]{1,0:T(8,128)S(1)} %add_select_fusion.1), channel_id=1, source_target_pairs={{0,128},{8,136},{16,144},{24,152},{32,160},{40,168},{48,176},{56,1... | collective-permute-start | bytes 3145736 | tf_op jit(solution)/shard_map/ppermute | solution.py:8
  226.6 25.9 %collective-permute-start.5 = (f32[1024,256]{1,0:T(8,128)S(1)}, f32[1024,256]{1,0:T(8,128)S(1)}, u32[]{:S(2)}, u32[]{:S(2)}) collective-permute-start(f32[1024,256]{1,0:T(8,128)S(1)} %add_select_fusion), channel_id=1, source_target_pairs={{0,256},{8,264},{16,272},{24,280},{32,288},{40,296},{48,304},{56,3... | collective-permute-start | bytes 3145736 | tf_op jit(solution)/shard_map/ppermute | solution.py:8
  254.4 498.6 %reduce-scatter.2.cloned.1.call-start = ((), (), s32[]{:S(2)}) async-start(), calls=%async_computation.2 | async-start | bytes 2129920 | tf_op jit(solution)/shard_map/reduce_scatter | solution.py:39
Sparse Core Ops, SparseCore 0:
  254.5 40.7 all-gather.1
  301.8 451.1 reduce-scatter.1
where the time goes:
time: 762 us; the launch traced here: 761 us
  waiting for transfers between devices  693 us (91%)
  starting transfers between devices  34.3 us (5%)
  matrix products  15.4 us (2%)
  between operations  14.2 us (2%)
    reduce_scatter x1, waiting for transfers between devices, shards(): lax.psum_scatter(jnp.dot(full_rows.T, sketch, precision=lax.Precision.HIG...  451 us
    ppermute x6, waiting for transfers between devices, from_partner(): lax.ppermute(x, axis, [(i, i ^ 1 << distance) for i in range(lax.axis_siz...  201 us
    all_gather x1, waiting for transfers between devices, shards(): full_rows = lax.all_gather(sketch, 'col', axis=1, tiled=True)  40.7 us
    ppermute x6, starting transfers between devices, from_partner(): lax.ppermute(x, axis, [(i, i ^ 1 << distance) for i in range(lax.axis_siz...  34 us
  transfers between devices with their start and end apart: 8, of which 8 were waited for; matrix products, arithmetic and copies ran while one was open for 0% of the time, Pallas kernels for 0%

commit v1 on v0

v1 whole, which is shorter than its diff:
```python
import functools

import jax
import jax.numpy as jnp
import numpy as np
from jax import lax
from jax.experimental import pallas as pl
from jax.experimental.pallas import tpu as pltpu
from jax.sharding import PartitionSpec as P

F32 = jnp.float32
BF16 = jnp.bfloat16
GROUPS = 64
LANES = 512
VMEM_LIMIT = 48 * 1024 * 1024


def sylvester(order):
    both = np.arange(order)[:, None] & np.arange(order)[None, :]
    parity = np.zeros_like(both)
    while both.any():
        parity ^= both & 1
        both >>= 1
    return (1 - 2 * parity).astype(np.float32)


def split(x):
    high = x.astype(BF16)
    return high, (x - high.astype(F32)).astype(BF16)


def dot(a, b):
    return jnp.dot(a, b, preferred_element_type=F32)


def chunk_kernel(matrix_ref, signs_ref, out_ref):
    signed = (matrix_ref[...] * signs_ref[...].astype(F32)).T
    for half in range(2):
        for v in range(4):
            start = half * LANES + v * 128
            for q in range(4):
                out_ref[pl.ds(v * 8 + half * 4 + q, GROUPS, stride=32), :] = signed[
                    q * GROUPS : (q + 1) * GROUPS, start : start + 128
                ]


def mix_kernel(chunks_ref, block_table_ref, lane_table_ref, picks_ref, out_ref, mixed):
    received = jnp.concatenate(
        [chunks_ref[:, v * 8 : v * 8 + 8, :].reshape(8 * GROUPS, 128) for v in range(4)], axis=1
    )
    high, low = split(received)
    table = block_table_ref[...]
    high, low = split(dot(table, high) + dot(table, low))
    table = lane_table_ref[...]
    mixed[...] = (dot(high, table) + dot(low, table)) * F32(2.0**-8)
    first = lax.broadcasted_iota(jnp.int32, (8, 128), 0) < 4

    def eight(group, carry):
        base = pl.multiple_of(group * 8, 8)
        owner = base + lax.broadcasted_iota(jnp.int32, (8, 256), 0)
        local_picks = picks_ref[pl.ds(base, 8), :] - owner * 1024
        for inner in range(8):
            rows = pl.ds(pl.multiple_of((base + inner) * 8, 8), 8)
            sources = [mixed[rows, v * 128 : v * 128 + 128] for v in range(4)]
            found = []
            for part in range(2):
                local = jnp.broadcast_to(
                    local_picks[inner : inner + 1, part * 128 : part * 128 + 128], (8, 128)
                )
                lane = jnp.bitwise_and(local, 127)
                vreg = jnp.bitwise_and(jnp.right_shift(local, 7), 3)
                got = None
                for v in range(4):
                    here = jnp.take_along_axis(sources[v], lane, axis=1)
                    got = here if got is None else jnp.where(vreg == v, here, got)
                found.append((got, jnp.right_shift(local, 9) == 1))
            (a, up_a), (b, up_b) = found
            out_ref[rows, :] = jnp.where(
                first,
                jnp.where(up_a, pltpu.roll(a, 4, 0), a),
                jnp.where(up_b, b, pltpu.roll(b, 4, 0)),
            )
        return carry

    lax.fori_loop(0, GROUPS // 8, eight, 0)


def order_kernel(got_ref, across_ref, sketch_ref):
    for q in range(4):
        for part in range(2):
            across_ref[q * GROUPS : (q + 1) * GROUPS, part * 128 : part * 128 + 128] = got_ref[
                pl.ds(part * 4 + q, GROUPS, stride=8), :
            ]
    sketch_ref[...] = across_ref[...].T


def gram_kernel(order, me_ref, sketch_ref, *refs):
    parts, out_ref = refs[:-1], refs[-1]
    me = me_ref[0]
    right_high, right_low = split(sketch_ref[...])
    width = sketch_ref.shape[1]
    block = 0
    for part in parts:
        for piece in range(part.shape[0] // width):
            left_high, left_low = split(part[piece * width : (piece + 1) * width, :])
            product = dot(left_high, right_high) + dot(left_high, right_low) + dot(left_low, right_high)
            place = pl.multiple_of(jnp.bitwise_xor(me, order[block]) * width, width)
            out_ref[pl.ds(place, width), :] = product
            block += 1


def call(kernel, out_shape, scratch=(), **more):
    vmem = pl.BlockSpec(memory_space=pltpu.VMEM)
    many = isinstance(out_shape, (list, tuple))
    return pl.pallas_call(
        kernel,
        out_shape=out_shape,
        out_specs=[vmem] * len(out_shape) if many else vmem,
        scratch_shapes=list(scratch),
        compiler_params=pltpu.CompilerParams(vmem_limit_bytes=VMEM_LIMIT),
        **more,
    )


def shape(*dims):
    return jax.ShapeDtypeStruct(dims, F32)


def from_partner(x, axis, distance):
    return lax.ppermute(x, axis, [(i, i ^ distance) for i in range(lax.axis_size(axis))])


def shards(matrix, signs, picks):
    all_picks = lax.all_gather(picks, "row", axis=0, tiled=False)
    chunks = call(chunk_kernel, shape(32 * GROUPS, 128))(matrix, signs[:, None])
    chunks = lax.all_to_all(chunks.reshape(GROUPS, 32, 128), "row", 0, 0, tiled=True)
    block_table = jnp.asarray(np.kron(sylvester(2 * GROUPS), np.eye(4)), BF16)
    lane_table = jnp.asarray(sylvester(LANES), BF16)
    picked = call(mix_kernel, shape(8 * GROUPS, 128), [pltpu.VMEM((8 * GROUPS, LANES), F32)])(
        chunks, block_table, lane_table, all_picks
    )
    picked = lax.all_to_all(picked, "row", 0, 0, tiled=True)
    across, sketch = call(order_kernel, [shape(256, 256), shape(256, 256)])(picked)

    pieces = [across]
    for distance in (4, 2, 1):
        held = pieces[0] if len(pieces) == 1 else jnp.concatenate(pieces, 0)
        pieces.append(from_partner(held, "col", distance))
    me = lax.axis_index("col").astype(jnp.int32)[None]
    vmem = pl.BlockSpec(memory_space=pltpu.VMEM)
    kernel = functools.partial(gram_kernel, (0, 4, 2, 6, 1, 5, 3, 7))
    gram = call(
        kernel,
        shape(2048, 256),
        in_specs=[pl.BlockSpec(memory_space=pltpu.SMEM)] + [vmem] * 5,
    )(me, sketch, *pieces)

    x_groups = [[x * 16 + i for x in range(4)] for i in range(16)]
    rest_groups = [[x * 16 + i for i in range(16)] for x in range(4)]
    gram = lax.all_to_all(gram, "row", 0, 0, axis_index_groups=x_groups, tiled=True)
    gram = jnp.sum(gram.reshape(4, 512, 256), 0)
    gram = lax.all_to_all(gram, "row", 0, 0, axis_index_groups=rest_groups, tiled=True)
    gram = jnp.sum(gram.reshape(16, 32, 256), 0) * F32(2.0**-14)
    return sketch, gram


def solution(mesh):
    placed = (P("row", "col"), P("row"), P("row"))
    return jax.shard_map(
        shards,
        mesh=mesh,
        in_specs=placed,
        out_specs=(P("row", "col"), P("row", "col")),
        check_vma=False,
    )
```

time: 762 us -> 364 us (0.48)
  the two profiles are of different devices: /device:TPU:8 before, /device:TPU:16 now
where the time goes in v1:
time: 364 us; the launch traced here: 363 us
  blocking collectives  310 us (85%)
  starting transfers between devices  25.9 us (7%)
  waiting for transfers between devices  17.1 us (5%)
  Pallas kernels  6.78 us (2%)
    all_gather x1, blocking collectives, shards(): all_picks = lax.all_gather(picks, 'row', axis=0, tiled=False)  233 us
    all_to_all x1, blocking collectives, shards(): lax.all_to_all(gram, 'row', 0, 0, axis_index_groups=x_groups, tiled=True)  29.4 us
    all_to_all x1, blocking collectives, shards(): lax.all_to_all(gram, 'row', 0, 0, axis_index_groups=rest_groups, tiled=True)  24.5 us
    all_to_all x1, blocking collectives, shards(): picked = lax.all_to_all(picked, 'row', 0, 0, tiled=True)  22.5 us
    all_to_all x1, starting transfers between devices, shards(): lax.all_to_all(chunks.reshape(GROUPS, 32, 128), 'row', 0, 0, tiled=True)  17.2 us
    ppermute x3, waiting for transfers between devices, from_partner(): lax.ppermute(x, axis, [(i, i ^ distance) for i in range(lax.axis_size(axi...  17.1 us
    ppermute x3, starting transfers between devices, from_partner(): lax.ppermute(x, axis, [(i, i ^ distance) for i in range(lax.axis_size(axi...  8.61 us
  transfers between devices with their start and end apart: 4, of which 3 were waited for; matrix products, arithmetic and copies ran while one was open for 0% of the time, Pallas kernels for 0%

profile of v1, /device:TPU:16, one launch (start us, length us, event | category | flops | bytes accessed | tf_op | source)
XLA Modules:
  0.0 363.4 jit_solution(5450409034142207903)
XLA Ops:
  0.6 0.9 copy.9.signs_ref
  1.5 0.0 copy-start
  1.6 1.2 copy-done
  2.8 1.9 shard_map.68
  4.7 17.2 %all-to-all-start = ((f32[64,32,128]{2,1,0:T(8,128)}), f32[64,32,128]{2,1,0:T(8,128)S(1)}, u32[]{:S(2)}, u32[]{:S(2)}) async-start(f32[64,32,128]{2,1,0:T(8,128)} %bitcast.1), calls=%async_computation | async-start | bytes 2097152 | tf_op jit(solution)/shard_map/all_to_all | solution.py:136
  22.0 233.5 %all-gather.1 = s32[64,1,256]{2,1,0:T(1,128)S(1)} all-gather(s32[1,1,256]{2,1,0:T(1,128)S(1)} %bitcast.17), channel_id=2, replica_groups=mesh['row'=64,'col'=8] {'row'}, dimensions={0}, use_global_device_ids=true | all-gather | bytes 66560 | tf_op jit(solution)/shard_map/all_gather | solution.py:134
  255.5 0.0 all-to-all-done.chunks_ref
  255.5 0.0 copy-done.1
  255.5 0.0 copy-done.2
  255.5 2.9 shard_map.69
  258.4 22.5 %all_to_all.34 = f32[64,8,128]{2,1,0:T(8,128)S(1)} all-to-all(f32[64,8,128]{2,1,0:T(8,128)S(1)} %bitcast.12), channel_id=1, replica_groups=mesh['row'=64,'col'=8] {'row'}, dimensions={0} | all-to-all | bytes 524288 | tf_op jit(solution)/shard_map/all_to_all | solution.py:142
  280.9 0.9 shard_map.70
  281.8 2.0 collective-permute-start
  283.8 7.3 %collective-permute-done.refs_1_ = f32[256,256]{1,0:T(8,128)S(1)} collective-permute-done((f32[256,256]{1,0:T(8,128)S(1)}, f32[256,256]{1,0:T(8,128)S(1)}, u32[]{:S(2)}, u32[]{:S(2)}) %collective-permute-start) | collective-permute-done | bytes 262176 | tf_op jit(solution)/shard_map/ppermute | solution.py:130
  291.2 4.6 %collective-permute-start.1 = (f32[512,256]{1,0:T(8,128)S(1)}, f32[512,256]{1,0:T(8,128)S(1)}, u32[]{:S(2)}, u32[]{:S(2)}) collective-permute-start(f32[512,256]{1,0:T(8,128)S(1)} %pad_maximum_fusion.1), channel_id=1, source_target_pairs={{0,2},{1,3},{2,0},{3,1},{4,6},{5,7},{6,4},{7,5},{8,10},{9,11},{10,... | collective-permute-start | bytes 1572872 | tf_op jit(solution)/shard_map/ppermute | solution.py:130
  295.8 7.1 %collective-permute-done.1.refs_2_ = f32[512,256]{1,0:T(8,128)S(1)} collective-permute-done((f32[512,256]{1,0:T(8,128)S(1)}, f32[512,256]{1,0:T(8,128)S(1)}, u32[]{:S(2)}, u32[]{:S(2)}) %collective-permute-start.1) | collective-permute-done | bytes 524320 | tf_op jit(solution)/shard_map/ppermute | solution.py:130
  303.0 0.1 pad_maximum_fusion
  303.1 1.9 collective-permute-start.2
  305.0 2.6 collective-permute-done.2.refs_3_
  307.6 1.1 shard_map.71
  308.7 29.4 %all_to_all.35 = f32[4,512,256]{2,1,0:T(8,128)S(1)} all-to-all(f32[4,512,256]{2,1,0:T(8,128)S(1)} %bitcast.11), channel_id=1, replica_groups={{0,128,256,384},{8,136,264,392},{16,144,272,400},{24,152,280,408},{32,1..., dimensions={0} | all-to-all | bytes 4194304 | tf_op jit(solution)/shard_map/all_to_all | solution.py:160
  338.1 0.2 reduce_sum.18
  338.3 24.5 %all_to_all.36 = f32[16,32,256]{2,1,0:T(8,128)S(1)} all-to-all(f32[16,32,256]{2,1,0:T(8,128)S(1)} %bitcast.15), channel_id=1, replica_groups={{0,8,16,24,32,40,48,56,64,72,80,88,96,104,112,120},{128,136,144,152,160..., dimensions={0} | all-to-all | bytes 1048576 | tf_op jit(solution)/shard_map/all_to_all | solution.py:162
  362.8 0.6 broadcast_multiply_fusion
  (9 shorter events, 0.1 us)
Async XLA Ops:
  1.5 1.2 copy-start
  2.8 19.2 %copy-start.4 = (s32[256]{0:T(256)S(1)}, s32[256]{0:T(256)}, u32[]{:S(2)}) copy-start(s32[256]{0:T(256)} %param.7) | copy-start | bytes 3076
  2.8 252.7 %copy-start.1 = (bf16[512,512]{1,0:T(8,128)(2,1)S(1)}, bf16[512,512]{1,0:T(8,128)(2,1)}, u32[]{:S(2)}) copy-start(bf16[512,512]{1,0:T(8,128)(2,1)} %constant.13.clone.lane_table_ref) | copy-start | bytes 1572868
  2.8 252.7 %copy-start.2 = (bf16[512,512]{1,0:T(8,128)(2,1)S(1)}, bf16[512,512]{1,0:T(8,128)(2,1)}, u32[]{:S(2)}) copy-start(bf16[512,512]{1,0:T(8,128)(2,1)} %constant.12.clone.block_table_ref) | copy-start | bytes 1572868
  4.7 250.8 %all-to-all-start = ((f32[64,32,128]{2,1,0:T(8,128)}), f32[64,32,128]{2,1,0:T(8,128)S(1)}, u32[]{:S(2)}, u32[]{:S(2)}) async-start(f32[64,32,128]{2,1,0:T(8,128)} %bitcast.1), calls=%async_computation | async-start | bytes 2097152 | tf_op jit(solution)/shard_map/all_to_all | solution.py:136
  281.8 25.9 %copy-start.3 = (f32[256,256]{1,0:T(8,128)S(1)}, f32[256,256]{1,0:T(8,128)}, u32[]{:S(2)}) copy-start(f32[256,256]{1,0:T(8,128)} %get-tuple-element.2.sketch_ref) | copy-start | bytes 786436
  281.8 9.4 %collective-permute-start = (f32[256,256]{1,0:T(8,128)S(1)}, f32[256,256]{1,0:T(8,128)S(1)}, u32[]{:S(2)}, u32[]{:S(2)}) collective-permute-start(f32[256,256]{1,0:T(8,128)S(1)} %get-tuple-element.5.refs_0_), channel_id=1, source_target_pairs={{0,4},{1,5},{2,6},{3,7},{4,0},{5,1},{6,2},{7,3},{8,12},{9,13},{10,... | collective-permute-start | bytes 786440 | tf_op jit(solution)/shard_map/ppermute | solution.py:130
  291.2 11.8 %collective-permute-start.1 = (f32[512,256]{1,0:T(8,128)S(1)}, f32[512,256]{1,0:T(8,128)S(1)}, u32[]{:S(2)}, u32[]{:S(2)}) collective-permute-start(f32[512,256]{1,0:T(8,128)S(1)} %pad_maximum_fusion.1), channel_id=1, source_target_pairs={{0,2},{1,3},{2,0},{3,1},{4,6},{5,7},{6,4},{7,5},{8,10},{9,11},{10,... | collective-permute-start | bytes 1572872 | tf_op jit(solution)/shard_map/ppermute | solution.py:130
  303.1 4.6 %collective-permute-start.2 = (f32[1024,256]{1,0:T(8,128)S(1)}, f32[1024,256]{1,0:T(8,128)S(1)}, u32[]{:S(2)}, u32[]{:S(2)}) collective-permute-start(f32[1024,256]{1,0:T(8,128)S(1)} %pad_maximum_fusion), channel_id=1, source_target_pairs={{0,1},{1,0},{2,3},{3,2},{4,5},{5,4},{6,7},{7,6},{8,9},{9,8},{10,11... | collective-permute-start | bytes 3145736 | tf_op jit(solution)/shard_map/ppermute | solution.py:130

commit v2 on v1

--- a/solution.py
+++ b/solution.py
@@ -12,6 +12,7 @@
 BF16 = jnp.bfloat16
 GROUPS = 64
 LANES = 512
+CHUNK = 40
 VMEM_LIMIT = 48 * 1024 * 1024
 
 
@@ -33,18 +34,24 @@
     return jnp.dot(a, b, preferred_element_type=F32)
 
 
-def chunk_kernel(matrix_ref, signs_ref, out_ref):
+def chunk_kernel(matrix_ref, signs_ref, picks_ref, out_ref):
     signed = (matrix_ref[...] * signs_ref[...].astype(F32)).T
     for half in range(2):
         for v in range(4):
             start = half * LANES + v * 128
             for q in range(4):
-                out_ref[pl.ds(v * 8 + half * 4 + q, GROUPS, stride=32), :] = signed[
+                out_ref[pl.ds(v * 8 + half * 4 + q, GROUPS, stride=CHUNK), :] = signed[
                     q * GROUPS : (q + 1) * GROUPS, start : start + 128
                 ]
+    for part in range(8):
+        if part < 2:
+            row = picks_ref[:, part * 128 : part * 128 + 128].astype(F32)
+        else:
+            row = jnp.zeros((1, 128), F32)
+        out_ref[pl.ds(32 + part, GROUPS, stride=CHUNK), :] = jnp.broadcast_to(row, (GROUPS, 128))
 
 
-def mix_kernel(chunks_ref, block_table_ref, lane_table_ref, picks_ref, out_ref, mixed):
+def mix_kernel(chunks_ref, block_table_ref, lane_table_ref, out_ref, mixed):
     received = jnp.concatenate(
         [chunks_ref[:, v * 8 : v * 8 + 8, :].reshape(8 * GROUPS, 128) for v in range(4)], axis=1
     )
@@ -56,16 +63,15 @@
     first = lax.broadcasted_iota(jnp.int32, (8, 128), 0) < 4
 
     def eight(group, carry):
-        base = pl.multiple_of(group * 8, 8)
-        owner = base + lax.broadcasted_iota(jnp.int32, (8, 256), 0)
-        local_picks = picks_ref[pl.ds(base, 8), :] - owner * 1024
         for inner in range(8):
-            rows = pl.ds(pl.multiple_of((base + inner) * 8, 8), 8)
+            block = group * 8 + inner
+            rows = pl.ds(pl.multiple_of(block * 8, 8), 8)
+            local_picks = chunks_ref[block, 32:40, :].astype(jnp.int32)
             sources = [mixed[rows, v * 128 : v * 128 + 128] for v in range(4)]
             found = []
             for part in range(2):
                 local = jnp.broadcast_to(
-                    local_picks[inner : inner + 1, part * 128 : part * 128 + 128], (8, 128)
+                    local_picks[part : part + 1, :], (8, 128)
                 )
                 lane = jnp.bitwise_and(local, 127)
                 vreg = jnp.bitwise_and(jnp.right_shift(local, 7), 3)
@@ -131,13 +137,15 @@
 
 
 def shards(matrix, signs, picks):
-    all_picks = lax.all_gather(picks, "row", axis=0, tiled=False)
-    chunks = call(chunk_kernel, shape(32 * GROUPS, 128))(matrix, signs[:, None])
-    chunks = lax.all_to_all(chunks.reshape(GROUPS, 32, 128), "row", 0, 0, tiled=True)
+    offsets = picks - lax.axis_index("row") * matrix.shape[0]
+    chunks = call(chunk_kernel, shape(CHUNK * GROUPS, 128))(
+        matrix, signs[:, None], offsets[None, :]
+    )
+    chunks = lax.all_to_all(chunks.reshape(GROUPS, CHUNK, 128), "row", 0, 0, tiled=True)
     block_table = jnp.asarray(np.kron(sylvester(2 * GROUPS), np.eye(4)), BF16)
     lane_table = jnp.asarray(sylvester(LANES), BF16)
     picked = call(mix_kernel, shape(8 * GROUPS, 128), [pltpu.VMEM((8 * GROUPS, LANES), F32)])(
-        chunks, block_table, lane_table, all_picks
+        chunks, block_table, lane_table
     )
     picked = lax.all_to_all(picked, "row", 0, 0, tiled=True)
     across, sketch = call(order_kernel, [shape(256, 256), shape(256, 256)])(picked)

time: 364 us -> 178 us (0.49)
  the two profiles are of different devices: /device:TPU:16 before, /device:TPU:8 now
where the time goes in v2:
time: 178 us
  blocking collectives  138 us (78%)
  waiting for transfers between devices  20.3 us (11%)
  starting transfers between devices  9.35 us (5%)
  Pallas kernels  5.34 us (3%)
  local copies, waits for them, and re-layouts  2.14 us (1%)
    all_to_all x1, blocking collectives, shards(): lax.all_to_all(chunks.reshape(GROUPS, CHUNK, 128), 'row', 0, 0, tiled=True)  57.6 us
    all_to_all x1, blocking collectives, shards(): lax.all_to_all(gram, 'row', 0, 0, axis_index_groups=x_groups, tiled=True)  29.4 us
    all_to_all x1, blocking collectives, shards(): lax.all_to_all(gram, 'row', 0, 0, axis_index_groups=rest_groups, tiled=True)  29.3 us
    all_to_all x1, blocking collectives, shards(): picked = lax.all_to_all(picked, 'row', 0, 0, tiled=True)  21.9 us
    ppermute x3, waiting for transfers between devices, from_partner(): lax.ppermute(x, axis, [(i, i ^ distance) for i in range(lax.axis_size(axi...  20.3 us
    ppermute x3, starting transfers between devices, from_partner(): lax.ppermute(x, axis, [(i, i ^ distance) for i in range(lax.axis_size(axi...  9.35 us
  transfers between devices with their start and end apart: 3, of which 3 were waited for; matrix products, arithmetic and copies ran while one was open for 0% of the time, Pallas kernels for 0%

profile of v2, /device:TPU:8, one launch (start us, length us, event | category | flops | bytes accessed | tf_op | source)
XLA Modules:
  0.0 177.6 jit_solution(7877886415553750279)
XLA Ops:
  0.6 0.9 copy.8.signs_ref
  1.5 0.7 broadcast_subtract_fusion
  2.2 0.0 copy-start
  2.2 1.2 copy-done
  3.5 0.5 shard_map.68
  4.0 57.6 %all_to_all.34.chunks_ref = f32[64,40,128]{2,1,0:T(8,128)S(1)} all-to-all(f32[64,40,128]{2,1,0:T(8,128)S(1)} %bitcast.9), channel_id=1, replica_groups=mesh['row'=64,'col'=8] {'row'}, dimensions={0} | all-to-all | bytes 2621440 | tf_op jit(solution)/shard_map/all_to_all | solution.py:144
  61.5 0.0 copy-done.1
  61.5 0.0 copy-done.2
  61.5 2.9 %shard_map.69 = f32[512,128]{1,0:T(8,128)S(1)} custom-call(f32[64,40,128]{2,1,0:T(8,128)S(1)} %all_to_all.34.chunks_ref, bf16[512,512]{1,0:T(8,128)(2,1)S(1)} %copy-done.2, bf16[512,512]{1,0:T(8,128)(2,1)S(1)} %copy-done.1), custom_call_target="tpu_custom_call" | custom-call | tf_op jit(solution)/shard_map/pallas_call | solution.py:147
  64.5 21.9 %all_to_all.35 = f32[64,8,128]{2,1,0:T(8,128)S(1)} all-to-all(f32[64,8,128]{2,1,0:T(8,128)S(1)} %bitcast.10), channel_id=1, replica_groups=mesh['row'=64,'col'=8] {'row'}, dimensions={0} | all-to-all | bytes 524288 | tf_op jit(solution)/shard_map/all_to_all | solution.py:150
  86.3 0.9 shard_map.70
  87.2 2.0 %collective-permute-start = (f32[256,256]{1,0:T(8,128)S(1)}, f32[256,256]{1,0:T(8,128)S(1)}, u32[]{:S(2)}, u32[]{:S(2)}) collective-permute-start(f32[256,256]{1,0:T(8,128)S(1)} %get-tuple-element.5.refs_0_), channel_id=1, source_target_pairs={{0,4},{1,5},{2,6},{3,7},{4,0},{5,1},{6,2},{7,3},{8,12},{9,13},{10,... | collective-permute-start | bytes 786440 | tf_op jit(solution)/shard_map/ppermute | solution.py:136
  89.2 8.7 %collective-permute-done.refs_1_ = f32[256,256]{1,0:T(8,128)S(1)} collective-permute-done((f32[256,256]{1,0:T(8,128)S(1)}, f32[256,256]{1,0:T(8,128)S(1)}, u32[]{:S(2)}, u32[]{:S(2)}) %collective-permute-start) | collective-permute-done | bytes 262176 | tf_op jit(solution)/shard_map/ppermute | solution.py:136
  98.0 5.4 %collective-permute-start.1 = (f32[512,256]{1,0:T(8,128)S(1)}, f32[512,256]{1,0:T(8,128)S(1)}, u32[]{:S(2)}, u32[]{:S(2)}) collective-permute-start(f32[512,256]{1,0:T(8,128)S(1)} %pad_maximum_fusion.1), channel_id=1, source_target_pairs={{0,2},{1,3},{2,0},{3,1},{4,6},{5,7},{6,4},{7,5},{8,10},{9,11},{10,... | collective-permute-start | bytes 1572872 | tf_op jit(solution)/shard_map/ppermute | solution.py:136
  103.4 9.0 %collective-permute-done.1.refs_2_ = f32[512,256]{1,0:T(8,128)S(1)} collective-permute-done((f32[512,256]{1,0:T(8,128)S(1)}, f32[512,256]{1,0:T(8,128)S(1)}, u32[]{:S(2)}, u32[]{:S(2)}) %collective-permute-start.1) | collective-permute-done | bytes 524320 | tf_op jit(solution)/shard_map/ppermute | solution.py:136
  112.4 0.1 pad_maximum_fusion
  112.5 1.9 %collective-permute-start.2 = (f32[1024,256]{1,0:T(8,128)S(1)}, f32[1024,256]{1,0:T(8,128)S(1)}, u32[]{:S(2)}, u32[]{:S(2)}) collective-permute-start(f32[1024,256]{1,0:T(8,128)S(1)} %pad_maximum_fusion), channel_id=1, source_target_pairs={{0,1},{1,0},{2,3},{3,2},{4,5},{5,4},{6,7},{7,6},{8,9},{9,8},{10,11... | collective-permute-start | bytes 3145736 | tf_op jit(solution)/shard_map/ppermute | solution.py:136
  114.4 2.6 %collective-permute-done.2.refs_3_ = f32[1024,256]{1,0:T(8,128)S(1)} collective-permute-done((f32[1024,256]{1,0:T(8,128)S(1)}, f32[1024,256]{1,0:T(8,128)S(1)}, u32[]{:S(2)}, u32[]{:S(2)}) %collective-permute-start.2) | collective-permute-done | bytes 1048608 | tf_op jit(solution)/shard_map/ppermute | solution.py:136
  117.0 0.0 copy-done.3
  117.0 1.1 shard_map.71
  118.1 29.4 %all_to_all.36 = f32[4,512,256]{2,1,0:T(8,128)S(1)} all-to-all(f32[4,512,256]{2,1,0:T(8,128)S(1)} %bitcast.8), channel_id=1, replica_groups={{0,128,256,384},{8,136,264,392},{16,144,272,400},{24,152,280,408},{32,1..., dimensions={0} | all-to-all | bytes 4194304 | tf_op jit(solution)/shard_map/all_to_all | solution.py:168
  147.5 0.2 reduce_sum.18
  147.6 29.3 %all_to_all.37 = f32[16,32,256]{2,1,0:T(8,128)S(1)} all-to-all(f32[16,32,256]{2,1,0:T(8,128)S(1)} %bitcast.13), channel_id=1, replica_groups={{0,8,16,24,32,40,48,56,64,72,80,88,96,104,112,120},{128,136,144,152,160..., dimensions={0} | all-to-all | bytes 1048576 | tf_op jit(solution)/shard_map/all_to_all | solution.py:170
  177.0 0.6 broadcast_multiply_fusion
  (5 shorter events, 0.1 us)
Async XLA Ops:
  2.2 1.2 copy-start
  3.5 58.1 %copy-start.1 = (bf16[512,512]{1,0:T(8,128)(2,1)S(1)}, bf16[512,512]{1,0:T(8,128)(2,1)}, u32[]{:S(2)}) copy-start(bf16[512,512]{1,0:T(8,128)(2,1)} %constant.20.clone.lane_table_ref) | copy-start | bytes 1572868
  3.5 58.1 %copy-start.2 = (bf16[512,512]{1,0:T(8,128)(2,1)S(1)}, bf16[512,512]{1,0:T(8,128)(2,1)}, u32[]{:S(2)}) copy-start(bf16[512,512]{1,0:T(8,128)(2,1)} %constant.19.clone.block_table_ref) | copy-start | bytes 1572868
  87.2 29.8 %copy-start.3 = (f32[256,256]{1,0:T(8,128)S(1)}, f32[256,256]{1,0:T(8,128)}, u32[]{:S(2)}) copy-start(f32[256,256]{1,0:T(8,128)} %get-tuple-element.2.sketch_ref) | copy-start | bytes 786436
  87.2 10.8 %collective-permute-start = (f32[256,256]{1,0:T(8,128)S(1)}, f32[256,256]{1,0:T(8,128)S(1)}, u32[]{:S(2)}, u32[]{:S(2)}) collective-permute-start(f32[256,256]{1,0:T(8,128)S(1)} %get-tuple-element.5.refs_0_), channel_id=1, source_target_pairs={{0,4},{1,5},{2,6},{3,7},{4,0},{5,1},{6,2},{7,3},{8,12},{9,13},{10,... | collective-permute-start | bytes 786440 | tf_op jit(solution)/shard_map/ppermute | solution.py:136
  98.0 14.4 %collective-permute-start.1 = (f32[512,256]{1,0:T(8,128)S(1)}, f32[512,256]{1,0:T(8,128)S(1)}, u32[]{:S(2)}, u32[]{:S(2)}) collective-permute-start(f32[512,256]{1,0:T(8,128)S(1)} %pad_maximum_fusion.1), channel_id=1, source_target_pairs={{0,2},{1,3},{2,0},{3,1},{4,6},{5,7},{6,4},{7,5},{8,10},{9,11},{10,... | collective-permute-start | bytes 1572872 | tf_op jit(solution)/shard_map/ppermute | solution.py:136
  112.5 4.6 %collective-permute-start.2 = (f32[1024,256]{1,0:T(8,128)S(1)}, f32[1024,256]{1,0:T(8,128)S(1)}, u32[]{:S(2)}, u32[]{:S(2)}) collective-permute-start(f32[1024,256]{1,0:T(8,128)S(1)} %pad_maximum_fusion), channel_id=1, source_target_pairs={{0,1},{1,0},{2,3},{3,2},{4,5},{5,4},{6,7},{7,6},{8,9},{9,8},{10,11... | collective-permute-start | bytes 3145736 | tf_op jit(solution)/shard_map/ppermute | solution.py:136

commit v3 on v1

--- a/solution.py
+++ b/solution.py
@@ -12,6 +12,7 @@
 BF16 = jnp.bfloat16
 GROUPS = 64
 LANES = 512
+TILES = 17
 VMEM_LIMIT = 48 * 1024 * 1024
 
 
@@ -33,40 +34,49 @@
     return jnp.dot(a, b, preferred_element_type=F32)
 
 
-def chunk_kernel(matrix_ref, signs_ref, out_ref):
-    signed = (matrix_ref[...] * signs_ref[...].astype(F32)).T
+def chunk_kernel(matrix_ref, signs_ref, picks_ref, out_ref):
+    signed = matrix_ref[...].T * signs_ref[...].astype(F32)
     for half in range(2):
         for v in range(4):
             start = half * LANES + v * 128
             for q in range(4):
-                out_ref[pl.ds(v * 8 + half * 4 + q, GROUPS, stride=32), :] = signed[
+                out_ref[pl.ds(v * 4 + q, GROUPS, stride=TILES), half, :] = signed[
                     q * GROUPS : (q + 1) * GROUPS, start : start + 128
                 ]
+    offsets = jnp.bitwise_and(picks_ref[...], 1023).astype(F32)
+    for part in range(2):
+        out_ref[pl.ds(16, GROUPS, stride=TILES), part, :] = jnp.broadcast_to(
+            offsets[part : part + 1, :], (GROUPS, 128)
+        )
 
 
-def mix_kernel(chunks_ref, block_table_ref, lane_table_ref, picks_ref, out_ref, mixed):
-    received = jnp.concatenate(
-        [chunks_ref[:, v * 8 : v * 8 + 8, :].reshape(8 * GROUPS, 128) for v in range(4)], axis=1
-    )
-    high, low = split(received)
-    table = block_table_ref[...]
-    high, low = split(dot(table, high) + dot(table, low))
-    table = lane_table_ref[...]
-    mixed[...] = (dot(high, table) + dot(low, table)) * F32(2.0**-8)
-    first = lax.broadcasted_iota(jnp.int32, (8, 128), 0) < 4
+def mix_kernel(chunks_ref, block_table_ref, lane_table_ref, out_ref, *mixed):
+    block_table = block_table_ref[...]
+    lane_table = lane_table_ref[...]
+    for pair in range(2):
+        columns = []
+        for v in range(4):
+            rows = [
+                chunks_ref[pl.ds(v * 4 + q, GROUPS, stride=TILES), half, :]
+                for q in (2 * pair, 2 * pair + 1)
+                for half in range(2)
+            ]
+            columns.append(jnp.concatenate(rows, 0))
+        high, low = split(jnp.concatenate(columns, 1))
+        high, low = split(dot(block_table, high) + dot(block_table, low))
+        done = (dot(high, lane_table) + dot(low, lane_table)) * F32(2.0**-8)
+        for v in range(4):
+            mixed[v][pair * 256 : pair * 256 + 256, :] = done[:, v * 128 : v * 128 + 128]
+    even = jnp.bitwise_and(lax.broadcasted_iota(jnp.int32, (8, 128), 0), 1) == 0
 
     def eight(group, carry):
-        base = pl.multiple_of(group * 8, 8)
-        owner = base + lax.broadcasted_iota(jnp.int32, (8, 256), 0)
-        local_picks = picks_ref[pl.ds(base, 8), :] - owner * 1024
         for inner in range(8):
-            rows = pl.ds(pl.multiple_of((base + inner) * 8, 8), 8)
-            sources = [mixed[rows, v * 128 : v * 128 + 128] for v in range(4)]
+            block = group * 8 + inner
+            local_picks = chunks_ref[block * TILES + 16].astype(jnp.int32)
+            sources = [mixed[v][pl.ds(block, 8, stride=GROUPS), :] for v in range(4)]
             found = []
             for part in range(2):
-                local = jnp.broadcast_to(
-                    local_picks[inner : inner + 1, part * 128 : part * 128 + 128], (8, 128)
-                )
+                local = jnp.broadcast_to(local_picks[part : part + 1, :], (8, 128))
                 lane = jnp.bitwise_and(local, 127)
                 vreg = jnp.bitwise_and(jnp.right_shift(local, 7), 3)
                 got = None
@@ -75,10 +85,10 @@
                     got = here if got is None else jnp.where(vreg == v, here, got)
                 found.append((got, jnp.right_shift(local, 9) == 1))
             (a, up_a), (b, up_b) = found
-            out_ref[rows, :] = jnp.where(
-                first,
-                jnp.where(up_a, pltpu.roll(a, 4, 0), a),
-                jnp.where(up_b, b, pltpu.roll(b, 4, 0)),
+            out_ref[pl.ds(pl.multiple_of(block * 8, 8), 8), :] = jnp.where(
+                even,
+                jnp.where(up_a, pltpu.roll(a, 7, 0), a),
+                jnp.where(up_b, b, pltpu.roll(b, 1, 0)),
             )
         return carry
 
@@ -89,7 +99,7 @@
     for q in range(4):
         for part in range(2):
             across_ref[q * GROUPS : (q + 1) * GROUPS, part * 128 : part * 128 + 128] = got_ref[
-                pl.ds(part * 4 + q, GROUPS, stride=8), :
+                pl.ds(q * 2 + part, GROUPS, stride=8), :
             ]
     sketch_ref[...] = across_ref[...].T
 
@@ -131,15 +141,17 @@
 
 
 def shards(matrix, signs, picks):
-    all_picks = lax.all_gather(picks, "row", axis=0, tiled=False)
-    chunks = call(chunk_kernel, shape(32 * GROUPS, 128))(matrix, signs[:, None])
-    chunks = lax.all_to_all(chunks.reshape(GROUPS, 32, 128), "row", 0, 0, tiled=True)
-    block_table = jnp.asarray(np.kron(sylvester(2 * GROUPS), np.eye(4)), BF16)
+    chunks = call(chunk_kernel, shape(GROUPS * TILES, 2, 128))(
+        matrix, signs[None, :], picks.reshape(2, 128)
+    )
+    chunks = lax.all_to_all(chunks.reshape(GROUPS, TILES, 2, 128), "row", 0, 0, tiled=True)
+    block_table = jnp.asarray(np.kron(np.eye(2), sylvester(2 * GROUPS)), BF16)
     lane_table = jnp.asarray(sylvester(LANES), BF16)
-    picked = call(mix_kernel, shape(8 * GROUPS, 128), [pltpu.VMEM((8 * GROUPS, LANES), F32)])(
-        chunks, block_table, lane_table, all_picks
+    picked = call(mix_kernel, shape(8 * GROUPS, 128), [pltpu.VMEM((8 * GROUPS, 128), F32)] * 4)(
+        chunks.reshape(GROUPS * TILES, 2, 128), block_table, lane_table
     )
-    picked = lax.all_to_all(picked, "row", 0, 0, tiled=True)
+    picked = picked.reshape(GROUPS, 8, 128)
+    picked = lax.all_to_all(picked, "row", 0, 0, tiled=True).reshape(8 * GROUPS, 128)
     across, sketch = call(order_kernel, [shape(256, 256), shape(256, 256)])(picked)
 
     pieces = [across]

time: 364 us -> 174 us (0.48)
  the two profiles are of different devices: /device:TPU:16 before, /device:TPU:8 now
where the time goes in v3:
time: 174 us
  blocking collectives  134 us (77%)
  waiting for transfers between devices  20.3 us (12%)
  starting transfers between devices  9.34 us (5%)
  Pallas kernels  5.88 us (3%)
  local copies, waits for them, and re-layouts  2.59 us (1%)
    all_to_all x1, blocking collectives, shards(): lax.all_to_all(chunks.reshape(GROUPS, TILES, 2, 128), 'row', 0, 0, tiled=...  53.1 us
    all_to_all x1, blocking collectives, shards(): lax.all_to_all(gram, 'row', 0, 0, axis_index_groups=x_groups, tiled=True)  29.4 us
    all_to_all x1, blocking collectives, shards(): lax.all_to_all(gram, 'row', 0, 0, axis_index_groups=rest_groups, tiled=True)  29.3 us
    all_to_all x1, blocking collectives, shards(): lax.all_to_all(picked, 'row', 0, 0, tiled=True).reshape(8 * GROUPS, 128)  22.2 us
    ppermute x3, waiting for transfers between devices, from_partner(): lax.ppermute(x, axis, [(i, i ^ distance) for i in range(lax.axis_size(axi...  20.3 us
    ppermute x3, starting transfers between devices, from_partner(): lax.ppermute(x, axis, [(i, i ^ distance) for i in range(lax.axis_size(axi...  9.34 us
  transfers between devices with their start and end apart: 3, of which 3 were waited for; matrix products, arithmetic and copies ran while one was open for 0% of the time, Pallas kernels for 0%

profile of v3, /device:TPU:8, one launch (start us, length us, event | category | flops | bytes accessed | tf_op | source)
XLA Modules:
  0.0 173.7 jit_solution(12385790724401654438)
XLA Ops:
  0.6 0.0 copy-start
  0.6 1.2 copy-done
  1.9 0.7 copy-done.4
  2.5 0.7 copy-done.5
  3.2 0.7 shard_map.68
  3.9 53.1 %all_to_all.28 = f32[64,17,2,128]{3,2,1,0:T(2,128)S(1)} all-to-all(f32[64,17,2,128]{3,2,1,0:T(2,128)S(1)} %bitcast.11), channel_id=1, replica_groups=mesh['row'=64,'col'=8] {'row'}, dimensions={0} | all-to-all | bytes 2228224 | tf_op jit(solution)/shard_map/all_to_all | solution.py:147
  57.0 0.0 copy-done.1
  57.0 0.0 copy-done.3
  57.0 3.3 %shard_map.69 = f32[512,128]{1,0:T(8,128)S(1)} custom-call(f32[1088,2,128]{2,1,0:T(2,128)S(1)} %bitcast.10, bf16[256,256]{1,0:T(8,128)(2,1)S(1)} %copy-done.3, bf16[512,512]{1,0:T(8,128)(2,1)S(1)} %copy-done.1), custom_call_target="tpu_custom_call" | custom-call | tf_op jit(solution)/shard_map/pallas_call | solution.py:150
  60.3 22.2 %all_to_all.29 = f32[64,8,128]{2,1,0:T(8,128)S(1)} all-to-all(f32[64,8,128]{2,1,0:T(8,128)S(1)} %bitcast.13), channel_id=1, replica_groups=mesh['row'=64,'col'=8] {'row'}, dimensions={0} | all-to-all | bytes 524288 | tf_op jit(solution)/shard_map/all_to_all | solution.py:154
  82.5 0.9 shard_map.70
  83.3 2.0 %collective-permute-start = (f32[256,256]{1,0:T(8,128)S(1)}, f32[256,256]{1,0:T(8,128)S(1)}, u32[]{:S(2)}, u32[]{:S(2)}) collective-permute-start(f32[256,256]{1,0:T(8,128)S(1)} %get-tuple-element.5.refs_0_), channel_id=1, source_target_pairs={{0,4},{1,5},{2,6},{3,7},{4,0},{5,1},{6,2},{7,3},{8,12},{9,13},{10,... | collective-permute-start | bytes 786440 | tf_op jit(solution)/shard_map/ppermute | solution.py:140
  85.4 8.7 %collective-permute-done.refs_1_ = f32[256,256]{1,0:T(8,128)S(1)} collective-permute-done((f32[256,256]{1,0:T(8,128)S(1)}, f32[256,256]{1,0:T(8,128)S(1)}, u32[]{:S(2)}, u32[]{:S(2)}) %collective-permute-start) | collective-permute-done | bytes 262176 | tf_op jit(solution)/shard_map/ppermute | solution.py:140
  94.1 5.4 %collective-permute-start.1 = (f32[512,256]{1,0:T(8,128)S(1)}, f32[512,256]{1,0:T(8,128)S(1)}, u32[]{:S(2)}, u32[]{:S(2)}) collective-permute-start(f32[512,256]{1,0:T(8,128)S(1)} %pad_maximum_fusion.1), channel_id=1, source_target_pairs={{0,2},{1,3},{2,0},{3,1},{4,6},{5,7},{6,4},{7,5},{8,10},{9,11},{10,... | collective-permute-start | bytes 1572872 | tf_op jit(solution)/shard_map/ppermute | solution.py:140
  99.5 9.0 %collective-permute-done.1.refs_2_ = f32[512,256]{1,0:T(8,128)S(1)} collective-permute-done((f32[512,256]{1,0:T(8,128)S(1)}, f32[512,256]{1,0:T(8,128)S(1)}, u32[]{:S(2)}, u32[]{:S(2)}) %collective-permute-start.1) | collective-permute-done | bytes 524320 | tf_op jit(solution)/shard_map/ppermute | solution.py:140
  108.5 0.1 pad_maximum_fusion
  108.5 1.9 %collective-permute-start.2 = (f32[1024,256]{1,0:T(8,128)S(1)}, f32[1024,256]{1,0:T(8,128)S(1)}, u32[]{:S(2)}, u32[]{:S(2)}) collective-permute-start(f32[1024,256]{1,0:T(8,128)S(1)} %pad_maximum_fusion), channel_id=1, source_target_pairs={{0,1},{1,0},{2,3},{3,2},{4,5},{5,4},{6,7},{7,6},{8,9},{9,8},{10,11... | collective-permute-start | bytes 3145736 | tf_op jit(solution)/shard_map/ppermute | solution.py:140
  110.5 2.6 %collective-permute-done.2.refs_3_ = f32[1024,256]{1,0:T(8,128)S(1)} collective-permute-done((f32[1024,256]{1,0:T(8,128)S(1)}, f32[1024,256]{1,0:T(8,128)S(1)}, u32[]{:S(2)}, u32[]{:S(2)}) %collective-permute-start.2) | collective-permute-done | bytes 1048608 | tf_op jit(solution)/shard_map/ppermute | solution.py:140
  113.1 0.0 copy-done.2
  113.1 1.1 shard_map.71
  114.2 29.4 %all_to_all.30 = f32[4,512,256]{2,1,0:T(8,128)S(1)} all-to-all(f32[4,512,256]{2,1,0:T(8,128)S(1)} %bitcast.9), channel_id=1, replica_groups={{0,128,256,384},{8,136,264,392},{16,144,272,400},{24,152,280,408},{32,1..., dimensions={0} | all-to-all | bytes 4194304 | tf_op jit(solution)/shard_map/all_to_all | solution.py:172
  143.5 0.2 reduce_sum.18
  143.7 29.3 %all_to_all.31 = f32[16,32,256]{2,1,0:T(8,128)S(1)} all-to-all(f32[16,32,256]{2,1,0:T(8,128)S(1)} %bitcast.16), channel_id=1, replica_groups={{0,8,16,24,32,40,48,56,64,72,80,88,96,104,112,120},{128,136,144,152,160..., dimensions={0} | all-to-all | bytes 1048576 | tf_op jit(solution)/shard_map/all_to_all | solution.py:174
  173.1 0.6 broadcast_multiply_fusion
  (7 shorter events, 0.1 us)
Async XLA Ops:
  0.6 1.2 copy-start
  1.9 0.7 copy-start.4
  2.5 0.7 copy-start.5
  3.2 53.8 %copy-start.1 = (bf16[512,512]{1,0:T(8,128)(2,1)S(1)}, bf16[512,512]{1,0:T(8,128)(2,1)}, u32[]{:S(2)}) copy-start(bf16[512,512]{1,0:T(8,128)(2,1)} %constant.13.clone.lane_table_ref) | copy-start | bytes 1572868
  3.2 53.8 %copy-start.3 = (bf16[256,256]{1,0:T(8,128)(2,1)S(1)}, bf16[256,256]{1,0:T(8,128)(2,1)}, u32[]{:S(2)}) copy-start(bf16[256,256]{1,0:T(8,128)(2,1)} %constant.12.clone.block_table_ref) | copy-start | bytes 393220
  83.3 29.8 %copy-start.2 = (f32[256,256]{1,0:T(8,128)S(1)}, f32[256,256]{1,0:T(8,128)}, u32[]{:S(2)}) copy-start(f32[256,256]{1,0:T(8,128)} %get-tuple-element.2.sketch_ref) | copy-start | bytes 786436
  83.3 10.8 %collective-permute-start = (f32[256,256]{1,0:T(8,128)S(1)}, f32[256,256]{1,0:T(8,128)S(1)}, u32[]{:S(2)}, u32[]{:S(2)}) collective-permute-start(f32[256,256]{1,0:T(8,128)S(1)} %get-tuple-element.5.refs_0_), channel_id=1, source_target_pairs={{0,4},{1,5},{2,6},{3,7},{4,0},{5,1},{6,2},{7,3},{8,12},{9,13},{10,... | collective-permute-start | bytes 786440 | tf_op jit(solution)/shard_map/ppermute | solution.py:140
  94.1 14.3 %collective-permute-start.1 = (f32[512,256]{1,0:T(8,128)S(1)}, f32[512,256]{1,0:T(8,128)S(1)}, u32[]{:S(2)}, u32[]{:S(2)}) collective-permute-start(f32[512,256]{1,0:T(8,128)S(1)} %pad_maximum_fusion.1), channel_id=1, source_target_pairs={{0,2},{1,3},{2,0},{3,1},{4,6},{5,7},{6,4},{7,5},{8,10},{9,11},{10,... | collective-permute-start | bytes 1572872 | tf_op jit(solution)/shard_map/ppermute | solution.py:140
  108.5 4.6 %collective-permute-start.2 = (f32[1024,256]{1,0:T(8,128)S(1)}, f32[1024,256]{1,0:T(8,128)S(1)}, u32[]{:S(2)}, u32[]{:S(2)}) collective-permute-start(f32[1024,256]{1,0:T(8,128)S(1)} %pad_maximum_fusion), channel_id=1, source_target_pairs={{0,1},{1,0},{2,3},{3,2},{4,5},{5,4},{6,7},{7,6},{8,9},{9,8},{10,11... | collective-permute-start | bytes 3145736 | tf_op jit(solution)/shard_map/ppermute | solution.py:140

commit v4 on v3

--- a/solution.py
+++ b/solution.py
@@ -114,8 +114,11 @@
         for piece in range(part.shape[0] // width):
             left_high, left_low = split(part[piece * width : (piece + 1) * width, :])
             product = dot(left_high, right_high) + dot(left_high, right_low) + dot(left_low, right_high)
-            place = pl.multiple_of(jnp.bitwise_xor(me, order[block]) * width, width)
-            out_ref[pl.ds(place, width), :] = product
+            place = jnp.bitwise_xor(me, order[block])
+            place = jnp.right_shift(place, 1) * 512 + jnp.bitwise_and(place, 1) * 128
+            for z in range(4):
+                start = pl.multiple_of(place + (z % 2) * 256 + (z // 2) * 64, 64)
+                out_ref[pl.ds(start, 64), :] = product[z * 64 : z * 64 + 64]
             block += 1
 
 
@@ -167,12 +170,12 @@
         in_specs=[pl.BlockSpec(memory_space=pltpu.SMEM)] + [vmem] * 5,
     )(me, sketch, *pieces)
 
-    x_groups = [[x * 16 + i for x in range(4)] for i in range(16)]
-    rest_groups = [[x * 16 + i for i in range(16)] for x in range(4)]
-    gram = lax.all_to_all(gram, "row", 0, 0, axis_index_groups=x_groups, tiled=True)
-    gram = jnp.sum(gram.reshape(4, 512, 256), 0)
-    gram = lax.all_to_all(gram, "row", 0, 0, axis_index_groups=rest_groups, tiled=True)
-    gram = jnp.sum(gram.reshape(16, 32, 256), 0) * F32(2.0**-14)
+    near = [[x * 16 + h * 4 + l * 2 + y for x in range(4) for l in range(2)] for h in range(4) for y in range(2)]
+    far = [[x * 16 + h * 4 + l * 2 + y for h in range(4) for y in range(2)] for x in range(4) for l in range(2)]
+    gram = lax.all_to_all(gram, "row", 0, 0, axis_index_groups=near, tiled=True)
+    gram = jnp.sum(gram.reshape(8, 256, 256), 0)
+    gram = lax.all_to_all(gram, "row", 0, 0, axis_index_groups=far, tiled=True)
+    gram = jnp.sum(gram.reshape(8, 32, 256), 0) * F32(2.0**-14)
     return sketch, gram
 
 

time: 174 us -> 170 us (0.977)
  blocking collectives: 134 us -> 130 us
    all_to_all x2, blocking collectives: 58.7 us -> 54.5 us  [the longest x1 30.5 us: shards(): gram = lax.all_to_all(gram, 'row', 0, 0, axis_index_groups=near, tiled=True)]
where the time goes in v4:
time: 170 us; the launch traced here: 169 us
  blocking collectives  130 us (76%)
  waiting for transfers between devices  20.3 us (12%)
  starting transfers between devices  9.34 us (5%)
  Pallas kernels  5.87 us (3%)
  local copies, waits for them, and re-layouts  2.59 us (2%)
    all_to_all x1, blocking collectives, shards(): lax.all_to_all(chunks.reshape(GROUPS, TILES, 2, 128), 'row', 0, 0, tiled=...  53.1 us
    all_to_all x1, blocking collectives, shards(): gram = lax.all_to_all(gram, 'row', 0, 0, axis_index_groups=near, tiled=True)  30.5 us
    all_to_all x1, blocking collectives, shards(): gram = lax.all_to_all(gram, 'row', 0, 0, axis_index_groups=far, tiled=True)  24 us
    all_to_all x1, blocking collectives, shards(): lax.all_to_all(picked, 'row', 0, 0, tiled=True).reshape(8 * GROUPS, 128)  22.2 us
    ppermute x3, waiting for transfers between devices, from_partner(): lax.ppermute(x, axis, [(i, i ^ distance) for i in range(lax.axis_size(axi...  20.3 us
    ppermute x3, starting transfers between devices, from_partner(): lax.ppermute(x, axis, [(i, i ^ distance) for i in range(lax.axis_size(axi...  9.34 us
  transfers between devices with their start and end apart: 3, of which 3 were waited for; matrix products, arithmetic and copies ran while one was open for 0% of the time, Pallas kernels for 0%

profile of v4, /device:TPU:8, one launch (start us, length us, event | category | flops | bytes accessed | tf_op | source)
XLA Modules:
  0.0 169.4 jit_solution(2154294146873482180)
XLA Ops:
  0.6 0.0 copy-start
  0.6 1.2 copy-done
  1.9 0.7 copy-done.4
  2.5 0.7 copy-done.5
  3.2 0.7 shard_map.68
  3.9 53.1 %all_to_all.28 = f32[64,17,2,128]{3,2,1,0:T(2,128)S(1)} all-to-all(f32[64,17,2,128]{3,2,1,0:T(2,128)S(1)} %bitcast.11), channel_id=1, replica_groups=mesh['row'=64,'col'=8] {'row'}, dimensions={0} | all-to-all | bytes 2228224 | tf_op jit(solution)/shard_map/all_to_all | solution.py:150
  57.0 0.0 copy-done.1
  57.0 0.0 copy-done.3
  57.0 3.3 %shard_map.69 = f32[512,128]{1,0:T(8,128)S(1)} custom-call(f32[1088,2,128]{2,1,0:T(2,128)S(1)} %bitcast.10, bf16[256,256]{1,0:T(8,128)(2,1)S(1)} %copy-done.3, bf16[512,512]{1,0:T(8,128)(2,1)S(1)} %copy-done.1), custom_call_target="tpu_custom_call" | custom-call | tf_op jit(solution)/shard_map/pallas_call | solution.py:153
  60.3 22.2 %all_to_all.29 = f32[64,8,128]{2,1,0:T(8,128)S(1)} all-to-all(f32[64,8,128]{2,1,0:T(8,128)S(1)} %bitcast.13), channel_id=1, replica_groups=mesh['row'=64,'col'=8] {'row'}, dimensions={0} | all-to-all | bytes 524288 | tf_op jit(solution)/shard_map/all_to_all | solution.py:157
  82.5 0.9 shard_map.70
  83.3 2.0 %collective-permute-start = (f32[256,256]{1,0:T(8,128)S(1)}, f32[256,256]{1,0:T(8,128)S(1)}, u32[]{:S(2)}, u32[]{:S(2)}) collective-permute-start(f32[256,256]{1,0:T(8,128)S(1)} %get-tuple-element.5.refs_0_), channel_id=1, source_target_pairs={{0,4},{1,5},{2,6},{3,7},{4,0},{5,1},{6,2},{7,3},{8,12},{9,13},{10,... | collective-permute-start | bytes 786440 | tf_op jit(solution)/shard_map/ppermute | solution.py:143
  85.4 8.7 %collective-permute-done.refs_1_ = f32[256,256]{1,0:T(8,128)S(1)} collective-permute-done((f32[256,256]{1,0:T(8,128)S(1)}, f32[256,256]{1,0:T(8,128)S(1)}, u32[]{:S(2)}, u32[]{:S(2)}) %collective-permute-start) | collective-permute-done | bytes 262176 | tf_op jit(solution)/shard_map/ppermute | solution.py:143
  94.1 5.4 %collective-permute-start.1 = (f32[512,256]{1,0:T(8,128)S(1)}, f32[512,256]{1,0:T(8,128)S(1)}, u32[]{:S(2)}, u32[]{:S(2)}) collective-permute-start(f32[512,256]{1,0:T(8,128)S(1)} %pad_maximum_fusion.1), channel_id=1, source_target_pairs={{0,2},{1,3},{2,0},{3,1},{4,6},{5,7},{6,4},{7,5},{8,10},{9,11},{10,... | collective-permute-start | bytes 1572872 | tf_op jit(solution)/shard_map/ppermute | solution.py:143
  99.5 9.0 %collective-permute-done.1.refs_2_ = f32[512,256]{1,0:T(8,128)S(1)} collective-permute-done((f32[512,256]{1,0:T(8,128)S(1)}, f32[512,256]{1,0:T(8,128)S(1)}, u32[]{:S(2)}, u32[]{:S(2)}) %collective-permute-start.1) | collective-permute-done | bytes 524320 | tf_op jit(solution)/shard_map/ppermute | solution.py:143
  108.5 0.1 pad_maximum_fusion
  108.5 1.9 %collective-permute-start.2 = (f32[1024,256]{1,0:T(8,128)S(1)}, f32[1024,256]{1,0:T(8,128)S(1)}, u32[]{:S(2)}, u32[]{:S(2)}) collective-permute-start(f32[1024,256]{1,0:T(8,128)S(1)} %pad_maximum_fusion), channel_id=1, source_target_pairs={{0,1},{1,0},{2,3},{3,2},{4,5},{5,4},{6,7},{7,6},{8,9},{9,8},{10,11... | collective-permute-start | bytes 3145736 | tf_op jit(solution)/shard_map/ppermute | solution.py:143
  110.5 2.6 %collective-permute-done.2.refs_3_ = f32[1024,256]{1,0:T(8,128)S(1)} collective-permute-done((f32[1024,256]{1,0:T(8,128)S(1)}, f32[1024,256]{1,0:T(8,128)S(1)}, u32[]{:S(2)}, u32[]{:S(2)}) %collective-permute-start.2) | collective-permute-done | bytes 1048608 | tf_op jit(solution)/shard_map/ppermute | solution.py:143
  113.1 0.0 copy-done.2
  113.1 1.0 shard_map.71
  114.1 30.5 %all_to_all.30 = f32[8,256,256]{2,1,0:T(8,128)S(1)} all-to-all(f32[8,256,256]{2,1,0:T(8,128)S(1)} %bitcast.9), channel_id=1, replica_groups={{0,16,128,144,256,272,384,400},{8,24,136,152,264,280,392,408},{32,48,16..., dimensions={0} | all-to-all | bytes 4194304 | tf_op jit(solution)/shard_map/all_to_all | solution.py:175
  144.7 0.1 reduce_sum.18
  144.8 24.0 %all_to_all.31 = f32[8,32,256]{2,1,0:T(8,128)S(1)} all-to-all(f32[8,32,256]{2,1,0:T(8,128)S(1)} %bitcast.16), channel_id=1, replica_groups={{0,8,32,40,64,72,96,104},{16,24,48,56,80,88,112,120},{128,136,160,168,1..., dimensions={0} | all-to-all | bytes 524288 | tf_op jit(solution)/shard_map/all_to_all | solution.py:177
  168.8 0.6 broadcast_multiply_fusion
  (7 shorter events, 0.1 us)
Async XLA Ops:
  0.6 1.2 copy-start
  1.9 0.7 copy-start.4
  2.5 0.7 copy-start.5
  3.2 53.8 %copy-start.1 = (bf16[512,512]{1,0:T(8,128)(2,1)S(1)}, bf16[512,512]{1,0:T(8,128)(2,1)}, u32[]{:S(2)}) copy-start(bf16[512,512]{1,0:T(8,128)(2,1)} %constant.13.clone.lane_table_ref) | copy-start | bytes 1572868
  3.2 53.8 %copy-start.3 = (bf16[256,256]{1,0:T(8,128)(2,1)S(1)}, bf16[256,256]{1,0:T(8,128)(2,1)}, u32[]{:S(2)}) copy-start(bf16[256,256]{1,0:T(8,128)(2,1)} %constant.12.clone.block_table_ref) | copy-start | bytes 393220
  83.3 29.8 %copy-start.2 = (f32[256,256]{1,0:T(8,128)S(1)}, f32[256,256]{1,0:T(8,128)}, u32[]{:S(2)}) copy-start(f32[256,256]{1,0:T(8,128)} %get-tuple-element.2.sketch_ref) | copy-start | bytes 786436
  83.3 10.8 %collective-permute-start = (f32[256,256]{1,0:T(8,128)S(1)}, f32[256,256]{1,0:T(8,128)S(1)}, u32[]{:S(2)}, u32[]{:S(2)}) collective-permute-start(f32[256,256]{1,0:T(8,128)S(1)} %get-tuple-element.5.refs_0_), channel_id=1, source_target_pairs={{0,4},{1,5},{2,6},{3,7},{4,0},{5,1},{6,2},{7,3},{8,12},{9,13},{10,... | collective-permute-start | bytes 786440 | tf_op jit(solution)/shard_map/ppermute | solution.py:143
  94.1 14.3 %collective-permute-start.1 = (f32[512,256]{1,0:T(8,128)S(1)}, f32[512,256]{1,0:T(8,128)S(1)}, u32[]{:S(2)}, u32[]{:S(2)}) collective-permute-start(f32[512,256]{1,0:T(8,128)S(1)} %pad_maximum_fusion.1), channel_id=1, source_target_pairs={{0,2},{1,3},{2,0},{3,1},{4,6},{5,7},{6,4},{7,5},{8,10},{9,11},{10,... | collective-permute-start | bytes 1572872 | tf_op jit(solution)/shard_map/ppermute | solution.py:143
  108.5 4.6 %collective-permute-start.2 = (f32[1024,256]{1,0:T(8,128)S(1)}, f32[1024,256]{1,0:T(8,128)S(1)}, u32[]{:S(2)}, u32[]{:S(2)}) collective-permute-start(f32[1024,256]{1,0:T(8,128)S(1)} %pad_maximum_fusion), channel_id=1, source_target_pairs={{0,1},{1,0},{2,3},{3,2},{4,5},{5,4},{6,7},{7,6},{8,9},{9,8},{10,11... | collective-permute-start | bytes 3145736 | tf_op jit(solution)/shard_map/ppermute | solution.py:143

commit v5 on v4

--- a/solution.py
+++ b/solution.py
@@ -85,40 +85,49 @@
                     got = here if got is None else jnp.where(vreg == v, here, got)
                 found.append((got, jnp.right_shift(local, 9) == 1))
             (a, up_a), (b, up_b) = found
-            out_ref[pl.ds(pl.multiple_of(block * 8, 8), 8), :] = jnp.where(
+            picked = jnp.where(
                 even,
                 jnp.where(up_a, pltpu.roll(a, 7, 0), a),
                 jnp.where(up_b, b, pltpu.roll(b, 1, 0)),
             )
+            partner = group * 8 + (inner ^ 1)
+            out_ref[pl.ds(pl.multiple_of(block * 16, 8), 8), :] = picked
+            out_ref[pl.ds(pl.multiple_of(partner * 16 + 8, 8), 8), :] = picked
         return carry
 
     lax.fori_loop(0, GROUPS // 8, eight, 0)
 
 
-def order_kernel(got_ref, across_ref, sketch_ref):
-    for q in range(4):
-        for part in range(2):
-            across_ref[q * GROUPS : (q + 1) * GROUPS, part * 128 : part * 128 + 128] = got_ref[
-                pl.ds(q * 2 + part, GROUPS, stride=8), :
-            ]
-    sketch_ref[...] = across_ref[...].T
-
-
-def gram_kernel(order, me_ref, sketch_ref, *refs):
+def order_kernel(me_ref, got_ref, left_ref, sketch_ref, other_ref):
+    mine = me_ref[0] * (16 * 32)
+    for whose, target in enumerate((sketch_ref, other_ref)):
+        for q in range(4):
+            halves = []
+            for part in range(2):
+                place = whose * 8 + q * 2 + part
+                halves.append(got_ref[pl.ds(place, GROUPS, stride=16), :])
+                start = whose * 256 + part * 128
+                left_ref[q * 32 : q * 32 + 32, start : start + 128] = got_ref[
+                    pl.ds(mine + place, 32, stride=16), :
+                ]
+            target[:, q * GROUPS : (q + 1) * GROUPS] = jnp.concatenate(halves, 1).T
+
+
+def gram_kernel(order, me_ref, sketch_ref, other_ref, *refs):
     parts, out_ref = refs[:-1], refs[-1]
     me = me_ref[0]
-    right_high, right_low = split(sketch_ref[...])
-    width = sketch_ref.shape[1]
+    right_high, right_low = split(jnp.concatenate([sketch_ref[...], other_ref[...]], 0))
+    width = 128
     block = 0
     for part in parts:
         for piece in range(part.shape[0] // width):
             left_high, left_low = split(part[piece * width : (piece + 1) * width, :])
             product = dot(left_high, right_high) + dot(left_high, right_low) + dot(left_low, right_high)
-            place = jnp.bitwise_xor(me, order[block])
-            place = jnp.right_shift(place, 1) * 512 + jnp.bitwise_and(place, 1) * 128
-            for z in range(4):
-                start = pl.multiple_of(place + (z % 2) * 256 + (z // 2) * 64, 64)
-                out_ref[pl.ds(start, 64), :] = product[z * 64 : z * 64 + 64]
+            column = jnp.bitwise_xor(me, order[block])
+            place = jnp.right_shift(column, 1) * 256 + jnp.bitwise_and(column, 1) * 64
+            for q in range(4):
+                start = pl.multiple_of(place + (q % 2) * 128 + (q // 2) * 32, 32)
+                out_ref[pl.ds(start, 32), :] = product[q * 32 : q * 32 + 32]
             block += 1
 
 
@@ -150,32 +159,33 @@
     chunks = lax.all_to_all(chunks.reshape(GROUPS, TILES, 2, 128), "row", 0, 0, tiled=True)
     block_table = jnp.asarray(np.kron(np.eye(2), sylvester(2 * GROUPS)), BF16)
     lane_table = jnp.asarray(sylvester(LANES), BF16)
-    picked = call(mix_kernel, shape(8 * GROUPS, 128), [pltpu.VMEM((8 * GROUPS, 128), F32)] * 4)(
+    picked = call(mix_kernel, shape(16 * GROUPS, 128), [pltpu.VMEM((8 * GROUPS, 128), F32)] * 4)(
         chunks.reshape(GROUPS * TILES, 2, 128), block_table, lane_table
     )
-    picked = picked.reshape(GROUPS, 8, 128)
-    picked = lax.all_to_all(picked, "row", 0, 0, tiled=True).reshape(8 * GROUPS, 128)
-    across, sketch = call(order_kernel, [shape(256, 256), shape(256, 256)])(picked)
-
-    pieces = [across]
+    picked = picked.reshape(GROUPS, 16, 128)
+    picked = lax.all_to_all(picked, "row", 0, 0, tiled=True).reshape(16 * GROUPS, 128)
+
+    vmem = pl.BlockSpec(memory_space=pltpu.VMEM)
+    smem = pl.BlockSpec(memory_space=pltpu.SMEM)
+    y_high = jnp.bitwise_and(lax.axis_index("row"), 1).astype(jnp.int32)[None]
+    me = lax.axis_index("col").astype(jnp.int32)[None]
+    left, sketch, other = call(
+        order_kernel, [shape(128, 512), shape(256, 256), shape(256, 256)], in_specs=[smem, vmem]
+    )(y_high, picked)
+
+    pieces = [left]
     for distance in (4, 2, 1):
         held = pieces[0] if len(pieces) == 1 else jnp.concatenate(pieces, 0)
         pieces.append(from_partner(held, "col", distance))
-    me = lax.axis_index("col").astype(jnp.int32)[None]
-    vmem = pl.BlockSpec(memory_space=pltpu.VMEM)
     kernel = functools.partial(gram_kernel, (0, 4, 2, 6, 1, 5, 3, 7))
-    gram = call(
-        kernel,
-        shape(2048, 256),
-        in_specs=[pl.BlockSpec(memory_space=pltpu.SMEM)] + [vmem] * 5,
-    )(me, sketch, *pieces)
+    gram = call(kernel, shape(1024, 256), in_specs=[smem] + [vmem] * 6)(me, sketch, other, *pieces)
 
     near = [[x * 16 + h * 4 + l * 2 + y for x in range(4) for l in range(2)] for h in range(4) for y in range(2)]
-    far = [[x * 16 + h * 4 + l * 2 + y for h in range(4) for y in range(2)] for x in range(4) for l in range(2)]
+    far = [[x * 16 + h * 4 + l * 2 + y for h in range(4)] for x in range(4) for l in range(2) for y in range(2)]
     gram = lax.all_to_all(gram, "row", 0, 0, axis_index_groups=near, tiled=True)
-    gram = jnp.sum(gram.reshape(8, 256, 256), 0)
+    gram = jnp.sum(gram.reshape(8, 128, 256), 0)
     gram = lax.all_to_all(gram, "row", 0, 0, axis_index_groups=far, tiled=True)
-    gram = jnp.sum(gram.reshape(8, 32, 256), 0) * F32(2.0**-14)
+    gram = jnp.sum(gram.reshape(4, 32, 256), 0) * F32(2.0**-14)
     return sketch, gram
 
 

time: 170 us -> 157 us (0.924)
  the two profiles are of different devices: /device:TPU:8 before, /device:TPU:56 now
where the time goes in v5:
time: 157 us; the launch traced here: 156 us
  blocking collectives  80 us (51%)
  waiting for transfers between devices  44.5 us (28%)
  starting transfers between devices  19.6 us (12%)
  Pallas kernels  6.98 us (4%)
  local copies, waits for them, and re-layouts  2.6 us (2%)
  other arithmetic  1.77 us (1%)
    all_to_all x1, blocking collectives, shards(): lax.all_to_all(chunks.reshape(GROUPS, TILES, 2, 128), 'row', 0, 0, tiled=...  47.7 us
    ppermute x3, waiting for transfers between devices, from_partner(): lax.ppermute(x, axis, [(i, i ^ distance) for i in range(lax.axis_size(axi...  28.2 us
    all_to_all x1, blocking collectives, shards(): gram = lax.all_to_all(gram, 'row', 0, 0, axis_index_groups=near, tiled=True)  20.5 us
    all_to_all x1, waiting for transfers between devices, shards(): lax.all_to_all(picked, 'row', 0, 0, tiled=True).reshape(16 * GROUPS, 128)  16.3 us
    all_to_all x1, blocking collectives, shards(): gram = lax.all_to_all(gram, 'row', 0, 0, axis_index_groups=far, tiled=True)  11.7 us
    all_to_all x1, starting transfers between devices, shards(): lax.all_to_all(picked, 'row', 0, 0, tiled=True).reshape(16 * GROUPS, 128)  11.2 us
    ppermute x3, starting transfers between devices, from_partner(): lax.ppermute(x, axis, [(i, i ^ distance) for i in range(lax.axis_size(axi...  8.45 us
    pallas_call x1, Pallas kernels, shards(): call(mix_kernel, shape(16 * GROUPS, 128), [pltpu.VMEM((8 * GROUPS, 128),...  4.08 us
  transfers between devices with their start and end apart: 4, of which 4 were waited for; matrix products, arithmetic and copies ran while one was open for 0% of the time, Pallas kernels for 0%

profile of v5, /device:TPU:56, one launch (start us, length us, event | category | flops | bytes accessed | tf_op | source)
XLA Modules:
  0.0 156.2 jit_solution(10923362254453636459)
XLA Ops:
  0.6 1.2 copy-done
  1.9 0.7 copy-done.4
  2.5 0.7 copy-done.5
  3.2 0.7 shard_map.68
  3.9 0.0 copy-start.1
  3.9 0.0 copy-start.3
  4.0 47.7 %all_to_all.28 = f32[64,17,2,128]{3,2,1,0:T(2,128)S(1)} all-to-all(f32[64,17,2,128]{3,2,1,0:T(2,128)S(1)} %bitcast.11), channel_id=1, replica_groups=mesh['row'=64,'col'=8] {'row'}, dimensions={0} | all-to-all | bytes 2228224 | tf_op jit(solution)/shard_map/all_to_all | solution.py:159
  51.7 4.1 %shard_map.69 = f32[1024,128]{1,0:T(8,128)} custom-call(f32[1088,2,128]{2,1,0:T(2,128)S(1)} %bitcast.10, bf16[256,256]{1,0:T(8,128)(2,1)S(1)} %copy-done.3, bf16[512,512]{1,0:T(8,128)(2,1)S(1)} %copy-done.1), custom_call_target="tpu_custom_call" | custom-call | tf_op jit(solution)/shard_map/pallas_call | solution.py:162
  55.8 11.2 %all-to-all-start.1 = ((f32[64,16,128]{2,1,0:T(8,128)}), f32[64,16,128]{2,1,0:T(8,128)S(1)}, u32[]{:S(2)}, u32[]{:S(2)}) async-start(f32[64,16,128]{2,1,0:T(8,128)} %bitcast.5), calls=%async_computation.1 | async-start | bytes 1048576 | tf_op jit(solution)/shard_map/all_to_all | solution.py:166
  67.0 16.3 %all-to-all-done.1 = f32[64,16,128]{2,1,0:T(8,128)S(1)} async-done(((f32[64,16,128]{2,1,0:T(8,128)}), f32[64,16,128]{2,1,0:T(8,128)S(1)}, u32[]{:S(2)}, u32[]{:S(2)}) %all-to-all-start.1) | async-done | bytes 524320 | tf_op jit(solution)/shard_map/all_to_all | solution.py:166
  83.3 1.2 shard_map.70
  84.5 4.5 %collective-permute-start = (f32[128,512]{1,0:T(8,128)S(1)}, f32[128,512]{1,0:T(8,128)S(1)}, u32[]{:S(2)}, u32[]{:S(2)}) collective-permute-start(f32[128,512]{1,0:T(8,128)S(1)} %get-tuple-element.7.refs_0_), channel_id=1, source_target_pairs={{0,4},{1,5},{2,6},{3,7},{4,0},{5,1},{6,2},{7,3},{8,12},{9,13},{10,... | collective-permute-start | bytes 786440 | tf_op jit(solution)/shard_map/ppermute | solution.py:152
  89.0 11.5 %collective-permute-done.refs_1_ = f32[128,512]{1,0:T(8,128)S(1)} collective-permute-done((f32[128,512]{1,0:T(8,128)S(1)}, f32[128,512]{1,0:T(8,128)S(1)}, u32[]{:S(2)}, u32[]{:S(2)}) %collective-permute-start) | collective-permute-done | bytes 262176 | tf_op jit(solution)/shard_map/ppermute | solution.py:152
  100.5 0.0 copy-start.2
  100.5 2.1 %collective-permute-start.1 = (f32[256,512]{1,0:T(8,128)S(1)}, f32[256,512]{1,0:T(8,128)S(1)}, u32[]{:S(2)}, u32[]{:S(2)}) collective-permute-start(f32[256,512]{1,0:T(8,128)S(1)} %pad_maximum_fusion.1), channel_id=1, source_target_pairs={{0,2},{1,3},{2,0},{3,1},{4,6},{5,7},{6,4},{7,5},{8,10},{9,11},{10,... | collective-permute-start | bytes 1572872 | tf_op jit(solution)/shard_map/ppermute | solution.py:152
  102.6 13.8 %collective-permute-done.1.refs_2_ = f32[256,512]{1,0:T(8,128)S(1)} collective-permute-done((f32[256,512]{1,0:T(8,128)S(1)}, f32[256,512]{1,0:T(8,128)S(1)}, u32[]{:S(2)}, u32[]{:S(2)}) %collective-permute-start.1) | collective-permute-done | bytes 524320 | tf_op jit(solution)/shard_map/ppermute | solution.py:152
  116.4 1.0 pad_maximum_fusion
  117.4 1.9 %collective-permute-start.2 = (f32[512,512]{1,0:T(8,128)}, f32[512,512]{1,0:T(8,128)S(1)}, u32[]{:S(2)}, u32[]{:S(2)}) collective-permute-start(f32[512,512]{1,0:T(8,128)} %pad_maximum_fusion), channel_id=1, source_target_pairs={{0,1},{1,0},{2,3},{3,2},{4,5},{5,4},{6,7},{7,6},{8,9},{9,8},{10,11... | collective-permute-start | bytes 3145736 | tf_op jit(solution)/shard_map/ppermute | solution.py:152
  119.4 2.8 %collective-permute-done.2.refs_3_ = f32[512,512]{1,0:T(8,128)S(1)} collective-permute-done((f32[512,512]{1,0:T(8,128)}, f32[512,512]{1,0:T(8,128)S(1)}, u32[]{:S(2)}, u32[]{:S(2)}) %collective-permute-start.2) | collective-permute-done | bytes 1048608 | tf_op jit(solution)/shard_map/ppermute | solution.py:152
  122.2 1.0 shard_map.71
  123.2 20.5 %all_to_all.29 = f32[8,128,256]{2,1,0:T(8,128)S(1)} all-to-all(f32[8,128,256]{2,1,0:T(8,128)S(1)} %bitcast.12), channel_id=1, replica_groups={{0,16,128,144,256,272,384,400},{8,24,136,152,264,280,392,408},{32,48,16..., dimensions={0} | all-to-all | bytes 2097152 | tf_op jit(solution)/shard_map/all_to_all | solution.py:185
  143.8 0.1 reduce_sum.18
  143.8 11.7 %all_to_all.30 = f32[4,32,256]{2,1,0:T(8,128)S(1)} all-to-all(f32[4,32,256]{2,1,0:T(8,128)S(1)} %bitcast.16), channel_id=1, replica_groups={{0,32,64,96},{8,40,72,104},{16,48,80,112},{24,56,88,120},{128,160,192,2..., dimensions={0} | all-to-all | bytes 262144 | tf_op jit(solution)/shard_map/all_to_all | solution.py:187
  155.6 0.6 broadcast_multiply_fusion
  (8 shorter events, 0.1 us)
Async XLA Ops:
  0.6 1.2 copy-start
  1.9 0.7 copy-start.4
  2.5 0.7 copy-start.5
  3.9 47.7 %copy-start.1 = (bf16[512,512]{1,0:T(8,128)(2,1)S(1)}, bf16[512,512]{1,0:T(8,128)(2,1)}, u32[]{:S(2)}) copy-start(bf16[512,512]{1,0:T(8,128)(2,1)} %constant.20.clone.lane_table_ref) | copy-start | bytes 1572868
  3.9 47.7 %copy-start.3 = (bf16[256,256]{1,0:T(8,128)(2,1)S(1)}, bf16[256,256]{1,0:T(8,128)(2,1)}, u32[]{:S(2)}) copy-start(bf16[256,256]{1,0:T(8,128)(2,1)} %constant.19.clone.block_table_ref) | copy-start | bytes 393220
  55.8 27.5 %all-to-all-start.1 = ((f32[64,16,128]{2,1,0:T(8,128)}), f32[64,16,128]{2,1,0:T(8,128)S(1)}, u32[]{:S(2)}, u32[]{:S(2)}) async-start(f32[64,16,128]{2,1,0:T(8,128)} %bitcast.5), calls=%async_computation.1 | async-start | bytes 1048576 | tf_op jit(solution)/shard_map/all_to_all | solution.py:166
  84.5 16.0 %collective-permute-start = (f32[128,512]{1,0:T(8,128)S(1)}, f32[128,512]{1,0:T(8,128)S(1)}, u32[]{:S(2)}, u32[]{:S(2)}) collective-permute-start(f32[128,512]{1,0:T(8,128)S(1)} %get-tuple-element.7.refs_0_), channel_id=1, source_target_pairs={{0,4},{1,5},{2,6},{3,7},{4,0},{5,1},{6,2},{7,3},{8,12},{9,13},{10,... | collective-permute-start | bytes 786440 | tf_op jit(solution)/shard_map/ppermute | solution.py:152
  100.5 21.7 %copy-start.2 = (f32[256,256]{1,0:T(8,128)S(1)}, f32[256,256]{1,0:T(8,128)}, u32[]{:S(2)}) copy-start(f32[256,256]{1,0:T(8,128)} %get-tuple-element.3.sketch_ref) | copy-start | bytes 786436
  100.5 15.9 %collective-permute-start.1 = (f32[256,512]{1,0:T(8,128)S(1)}, f32[256,512]{1,0:T(8,128)S(1)}, u32[]{:S(2)}, u32[]{:S(2)}) collective-permute-start(f32[256,512]{1,0:T(8,128)S(1)} %pad_maximum_fusion.1), channel_id=1, source_target_pairs={{0,2},{1,3},{2,0},{3,1},{4,6},{5,7},{6,4},{7,5},{8,10},{9,11},{10,... | collective-permute-start | bytes 1572872 | tf_op jit(solution)/shard_map/ppermute | solution.py:152
  117.4 4.8 %collective-permute-start.2 = (f32[512,512]{1,0:T(8,128)}, f32[512,512]{1,0:T(8,128)S(1)}, u32[]{:S(2)}, u32[]{:S(2)}) collective-permute-start(f32[512,512]{1,0:T(8,128)} %pad_maximum_fusion), channel_id=1, source_target_pairs={{0,1},{1,0},{2,3},{3,2},{4,5},{5,4},{6,7},{7,6},{8,9},{9,8},{10,11... | collective-permute-start | bytes 3145736 | tf_op jit(solution)/shard_map/ppermute | solution.py:152

commit v6 on v5

--- a/solution.py
+++ b/solution.py
@@ -98,37 +98,42 @@
     lax.fori_loop(0, GROUPS // 8, eight, 0)
 
 
-def order_kernel(me_ref, got_ref, left_ref, sketch_ref, other_ref):
-    mine = me_ref[0] * (16 * 32)
+def order_kernel(y_high_ref, column_ref, got_ref, own_ref, up_ref, down_ref, far_ref, sketch_ref, other_ref):
+    column = column_ref[0]
+    ring = y_high_ref[0] * 4 + jnp.right_shift(column, 1)
+    far = 2 + 4 * jnp.bitwise_and(column, 1)
+    for step, target in ((0, own_ref), (1, up_ref), (7, down_ref), (far, far_ref)):
+        y_high = jnp.right_shift(jnp.bitwise_and(ring + step, 7), 2)
+        for whose in range(2):
+            for q in range(4):
+                for part in range(2):
+                    place = jnp.bitwise_xor(y_high_ref[0], whose) * 8 + (y_high * (16 * 32) + q * 2 + part)
+                    start = whose * 256 + part * 128
+                    target[q * 32 : q * 32 + 32, start : start + 128] = got_ref[pl.ds(place, 32, stride=16), :]
     for whose, target in enumerate((sketch_ref, other_ref)):
         for q in range(4):
-            halves = []
-            for part in range(2):
-                place = whose * 8 + q * 2 + part
-                halves.append(got_ref[pl.ds(place, GROUPS, stride=16), :])
-                start = whose * 256 + part * 128
-                left_ref[q * 32 : q * 32 + 32, start : start + 128] = got_ref[
-                    pl.ds(mine + place, 32, stride=16), :
-                ]
+            halves = [got_ref[pl.ds(whose * 8 + q * 2 + part, GROUPS, stride=16), :] for part in range(2)]
             target[:, q * GROUPS : (q + 1) * GROUPS] = jnp.concatenate(halves, 1).T
 
 
-def gram_kernel(order, me_ref, sketch_ref, other_ref, *refs):
+def gram_kernel(y_high_ref, column_ref, sketch_ref, other_ref, *refs):
     parts, out_ref = refs[:-1], refs[-1]
-    me = me_ref[0]
-    right_high, right_low = split(jnp.concatenate([sketch_ref[...], other_ref[...]], 0))
-    width = 128
-    block = 0
-    for part in parts:
-        for piece in range(part.shape[0] // width):
-            left_high, left_low = split(part[piece * width : (piece + 1) * width, :])
-            product = dot(left_high, right_high) + dot(left_high, right_low) + dot(left_low, right_high)
-            column = jnp.bitwise_xor(me, order[block])
-            place = jnp.right_shift(column, 1) * 256 + jnp.bitwise_and(column, 1) * 64
-            for q in range(4):
-                start = pl.multiple_of(place + (q % 2) * 128 + (q // 2) * 32, 32)
-                out_ref[pl.ds(start, 32), :] = product[q * 32 : q * 32 + 32]
-            block += 1
+    chip = jnp.right_shift(column_ref[0], 1)
+    core = jnp.bitwise_and(column_ref[0], 1)
+    first = y_high_ref[0] == 0
+    sketch, other = sketch_ref[...], other_ref[...]
+    right_high, right_low = split(
+        jnp.concatenate([jnp.where(first, sketch, other), jnp.where(first, other, sketch)], 0)
+    )
+    for block, part in enumerate(parts):
+        left_high, left_low = split(part[...])
+        product = dot(left_high, right_high) + dot(left_high, right_low) + dot(left_low, right_high)
+        chip_of = jnp.bitwise_and(chip + (0, 3, 1, 2)[block % 4], 3)
+        core_of = jnp.bitwise_xor(core, block // 4)
+        place = chip_of * 256 + core_of * 64
+        for q in range(4):
+            start = pl.multiple_of(place + (q % 2) * 128 + (q // 2) * 32, 32)
+            out_ref[pl.ds(start, 32), :] = product[q * 32 : q * 32 + 32]
 
 
 def call(kernel, out_shape, scratch=(), **more):
@@ -152,6 +157,14 @@
     return lax.ppermute(x, axis, [(i, i ^ distance) for i in range(lax.axis_size(axis))])
 
 
+def around_ring(x, steps):
+    pairs = []
+    for device in range(512):
+        rest, ring, core = device // 16, device // 2 % 8, device % 2
+        pairs.append((device, rest * 16 + (ring + steps[core]) % 8 * 2 + core))
+    return lax.ppermute(x, ("row", "col"), pairs)
+
+
 def shards(matrix, signs, picks):
     chunks = call(chunk_kernel, shape(GROUPS * TILES, 2, 128))(
         matrix, signs[None, :], picks.reshape(2, 128)
@@ -169,16 +182,21 @@
     smem = pl.BlockSpec(memory_space=pltpu.SMEM)
     y_high = jnp.bitwise_and(lax.axis_index("row"), 1).astype(jnp.int32)[None]
     me = lax.axis_index("col").astype(jnp.int32)[None]
-    left, sketch, other = call(
-        order_kernel, [shape(128, 512), shape(256, 256), shape(256, 256)], in_specs=[smem, vmem]
-    )(y_high, picked)
-
-    pieces = [left]
-    for distance in (4, 2, 1):
-        held = pieces[0] if len(pieces) == 1 else jnp.concatenate(pieces, 0)
-        pieces.append(from_partner(held, "col", distance))
-    kernel = functools.partial(gram_kernel, (0, 4, 2, 6, 1, 5, 3, 7))
-    gram = call(kernel, shape(1024, 256), in_specs=[smem] + [vmem] * 6)(me, sketch, other, *pieces)
+    own, up, down, far, sketch, other = call(
+        order_kernel,
+        [shape(128, 512)] * 4 + [shape(256, 256)] * 2,
+        in_specs=[smem, smem, vmem],
+    )(y_high, me, picked)
+    pieces = [
+        own,
+        around_ring(up, (1, 1)),
+        around_ring(down, (7, 7)),
+        around_ring(far, (2, 6)),
+    ]
+    pieces += [from_partner(piece, "col", 1) for piece in pieces]
+    gram = call(gram_kernel, shape(1024, 256), in_specs=[smem, smem] + [vmem] * 10)(
+        y_high, me, sketch, other, *pieces
+    )
 
     near = [[x * 16 + h * 4 + l * 2 + y for x in range(4) for l in range(2)] for h in range(4) for y in range(2)]
     far = [[x * 16 + h * 4 + l * 2 + y for h in range(4)] for x in range(4) for l in range(2) for y in range(2)]

time: 157 us -> 147 us (0.936)
  the two profiles are of different devices: /device:TPU:56 before, /device:TPU:8 now
where the time goes in v6:
time: 147 us; the launch traced here: 146 us
  blocking collectives  83.7 us (57%)
  waiting for transfers between devices  28.6 us (19%)
  starting transfers between devices  21.6 us (15%)
  Pallas kernels  7.3 us (5%)
  local copies, waits for them, and re-layouts  3.55 us (2%)
    all_to_all x1, blocking collectives, shards(): lax.all_to_all(chunks.reshape(GROUPS, TILES, 2, 128), 'row', 0, 0, tiled=...  53.2 us
    all_to_all x1, waiting for transfers between devices, shards(): lax.all_to_all(picked, 'row', 0, 0, tiled=True).reshape(16 * GROUPS, 128)  22.1 us
    all_to_all x1, blocking collectives, shards(): gram = lax.all_to_all(gram, 'row', 0, 0, axis_index_groups=near, tiled=True)  18.7 us
    all_to_all x1, blocking collectives, shards(): gram = lax.all_to_all(gram, 'row', 0, 0, axis_index_groups=far, tiled=True)  11.8 us
    ppermute x4, starting transfers between devices, from_partner(): lax.ppermute(x, axis, [(i, i ^ distance) for i in range(lax.axis_size(axi...  8.12 us
    ppermute x3, starting transfers between devices, around_ring(): return lax.ppermute(x, ('row', 'col'), pairs)  7.75 us
    all_to_all x1, starting transfers between devices, shards(): lax.all_to_all(picked, 'row', 0, 0, tiled=True).reshape(16 * GROUPS, 128)  5.7 us
    ppermute x3, waiting for transfers between devices, around_ring(): return lax.ppermute(x, ('row', 'col'), pairs)  4.97 us
  transfers between devices with their start and end apart: 8, of which 4 were waited for; matrix products, arithmetic and copies ran while one was open for 0% of the time, Pallas kernels for 0%

profile of v6, /device:TPU:8, one launch (start us, length us, event | category | flops | bytes accessed | tf_op | source)
XLA Modules:
  0.0 146.1 jit_solution(8820045247516934700)
XLA Ops:
  0.6 1.2 copy-done
  1.9 0.7 copy-done.4
  2.5 0.7 copy-done.5
  3.2 0.7 shard_map.68
  4.0 53.2 %all_to_all.28 = f32[64,17,2,128]{3,2,1,0:T(2,128)S(1)} all-to-all(f32[64,17,2,128]{3,2,1,0:T(2,128)S(1)} %bitcast.11), channel_id=1, replica_groups=mesh['row'=64,'col'=8] {'row'}, dimensions={0} | all-to-all | bytes 2228224 | tf_op jit(solution)/shard_map/all_to_all | solution.py:172
  57.1 4.1 %shard_map.69 = f32[1024,128]{1,0:T(8,128)} custom-call(f32[1088,2,128]{2,1,0:T(2,128)S(1)} %bitcast.10, bf16[256,256]{1,0:T(8,128)(2,1)S(1)} %copy-done.3, bf16[512,512]{1,0:T(8,128)(2,1)S(1)} %copy-done.1), custom_call_target="tpu_custom_call" | custom-call | tf_op jit(solution)/shard_map/pallas_call | solution.py:175
  61.2 5.7 %all-to-all-start.1 = ((f32[64,16,128]{2,1,0:T(8,128)}), f32[64,16,128]{2,1,0:T(8,128)S(1)}, u32[]{:S(2)}, u32[]{:S(2)}) async-start(f32[64,16,128]{2,1,0:T(8,128)} %bitcast.6), calls=%async_computation.1 | async-start | bytes 1048576 | tf_op jit(solution)/shard_map/all_to_all | solution.py:179
  66.9 22.1 %all-to-all-done.1 = f32[64,16,128]{2,1,0:T(8,128)S(1)} async-done(((f32[64,16,128]{2,1,0:T(8,128)}), f32[64,16,128]{2,1,0:T(8,128)S(1)}, u32[]{:S(2)}, u32[]{:S(2)}) %all-to-all-start.1) | async-done | bytes 524320 | tf_op jit(solution)/shard_map/all_to_all | solution.py:179
  89.0 1.4 shard_map.70
  90.5 2.0 %collective-permute-start = (f32[128,512]{1,0:T(8,128)S(1)}, f32[128,512]{1,0:T(8,128)S(1)}, u32[]{:S(2)}, u32[]{:S(2)}) collective-permute-start(f32[128,512]{1,0:T(8,128)S(1)} %get-tuple-element.11), channel_id=1, source_target_pairs={{0,2},{1,3},{2,4},{3,5},{4,6},{5,7},{6,8},{7,9},{8,10},{9,11},{10,... | collective-permute-start | bytes 786440 | tf_op jit(solution)/shard_map/ppermute | solution.py:165
  92.5 3.8 %collective-permute-start.1 = (f32[128,512]{1,0:T(8,128)S(1)}, f32[128,512]{1,0:T(8,128)S(1)}, u32[]{:S(2)}, u32[]{:S(2)}) collective-permute-start(f32[128,512]{1,0:T(8,128)S(1)} %get-tuple-element.12), channel_id=1, source_target_pairs={{0,14},{1,15},{2,0},{3,1},{4,2},{5,3},{6,4},{7,5},{8,6},{9,7},{10,... | collective-permute-start | bytes 786440 | tf_op jit(solution)/shard_map/ppermute | solution.py:165
  96.3 1.9 %collective-permute-start.2 = (f32[128,512]{1,0:T(8,128)S(1)}, f32[128,512]{1,0:T(8,128)S(1)}, u32[]{:S(2)}, u32[]{:S(2)}) collective-permute-start(f32[128,512]{1,0:T(8,128)S(1)} %get-tuple-element.13), channel_id=1, source_target_pairs={{0,4},{1,13},{2,6},{3,15},{4,8},{5,1},{6,10},{7,3},{8,12},{9,5},{1... | collective-permute-start | bytes 786440 | tf_op jit(solution)/shard_map/ppermute | solution.py:165
  98.3 1.9 %collective-permute-start.3 = (f32[128,512]{1,0:T(8,128)S(1)}, f32[128,512]{1,0:T(8,128)S(1)}, u32[]{:S(2)}, u32[]{:S(2)}) collective-permute-start(f32[128,512]{1,0:T(8,128)S(1)} %get-tuple-element.10.refs_0_), channel_id=1, source_target_pairs={{0,1},{1,0},{2,3},{3,2},{4,5},{5,4},{6,7},{7,6},{8,9},{9,8},{10,11... | collective-permute-start | bytes 786440 | tf_op jit(solution)/shard_map/ppermute | solution.py:157
  100.2 2.4 %collective-permute-start.4 = (f32[128,512]{1,0:T(8,128)S(1)}, f32[128,512]{1,0:T(8,128)S(1)}, u32[]{:S(2)}, u32[]{:S(2)}) collective-permute-start(f32[128,512]{1,0:T(8,128)S(1)} %collective-permute-done.refs_1_), channel_id=1, source_target_pairs={{0,1},{1,0},{2,3},{3,2},{4,5},{5,4},{6,7},{7,6},{8,9},{9,8},{10,11... | collective-permute-start | bytes 786440 | tf_op jit(solution)/shard_map/ppermute | solution.py:157
  102.6 3.8 %collective-permute-done.1.refs_2_ = f32[128,512]{1,0:T(8,128)S(1)} collective-permute-done((f32[128,512]{1,0:T(8,128)S(1)}, f32[128,512]{1,0:T(8,128)S(1)}, u32[]{:S(2)}, u32[]{:S(2)}) %collective-permute-start.1) | collective-permute-done | bytes 262176 | tf_op jit(solution)/shard_map/ppermute | solution.py:165
  106.4 1.9 %collective-permute-start.5 = (f32[128,512]{1,0:T(8,128)S(1)}, f32[128,512]{1,0:T(8,128)S(1)}, u32[]{:S(2)}, u32[]{:S(2)}) collective-permute-start(f32[128,512]{1,0:T(8,128)S(1)} %collective-permute-done.1.refs_2_), channel_id=1, source_target_pairs={{0,1},{1,0},{2,3},{3,2},{4,5},{5,4},{6,7},{7,6},{8,9},{9,8},{10,11... | collective-permute-start | bytes 786440 | tf_op jit(solution)/shard_map/ppermute | solution.py:157
  108.3 1.1 collective-permute-done.2.refs_3_
  109.5 1.9 %collective-permute-start.6 = (f32[128,512]{1,0:T(8,128)S(1)}, f32[128,512]{1,0:T(8,128)S(1)}, u32[]{:S(2)}, u32[]{:S(2)}) collective-permute-start(f32[128,512]{1,0:T(8,128)S(1)} %collective-permute-done.2.refs_3_), channel_id=1, source_target_pairs={{0,1},{1,0},{2,3},{3,2},{4,5},{5,4},{6,7},{7,6},{8,9},{9,8},{10,11... | collective-permute-start | bytes 786440 | tf_op jit(solution)/shard_map/ppermute | solution.py:157
  111.4 1.5 %collective-permute-done.6.refs_7_ = f32[128,512]{1,0:T(8,128)S(1)} collective-permute-done((f32[128,512]{1,0:T(8,128)S(1)}, f32[128,512]{1,0:T(8,128)S(1)}, u32[]{:S(2)}, u32[]{:S(2)}) %collective-permute-start.6) | collective-permute-done | bytes 262176 | tf_op jit(solution)/shard_map/ppermute | solution.py:157
  112.9 0.9 copy-done.2
  113.8 1.1 shard_map.71
  114.9 18.7 %all_to_all.29 = f32[8,128,256]{2,1,0:T(8,128)S(1)} all-to-all(f32[8,128,256]{2,1,0:T(8,128)S(1)} %bitcast.12), channel_id=1, replica_groups={{0,16,128,144,256,272,384,400},{8,24,136,152,264,280,392,408},{32,48,16..., dimensions={0} | all-to-all | bytes 2097152 | tf_op jit(solution)/shard_map/all_to_all | solution.py:203
  133.7 11.8 %all_to_all.30 = f32[4,32,256]{2,1,0:T(8,128)S(1)} all-to-all(f32[4,32,256]{2,1,0:T(8,128)S(1)} %bitcast.16), channel_id=1, replica_groups={{0,32,64,96},{8,40,72,104},{16,48,80,112},{24,56,88,120},{128,160,192,2..., dimensions={0} | all-to-all | bytes 262144 | tf_op jit(solution)/shard_map/all_to_all | solution.py:205
  145.5 0.6 broadcast_multiply_fusion
  (14 shorter events, 0.1 us)
Async XLA Ops:
  0.6 1.2 copy-start
  1.9 0.7 copy-start.4
  2.5 0.7 copy-start.5
  3.9 53.2 %copy-start.1 = (bf16[512,512]{1,0:T(8,128)(2,1)S(1)}, bf16[512,512]{1,0:T(8,128)(2,1)}, u32[]{:S(2)}) copy-start(bf16[512,512]{1,0:T(8,128)(2,1)} %constant.20.clone.lane_table_ref) | copy-start | bytes 1572868
  3.9 53.2 %copy-start.3 = (bf16[256,256]{1,0:T(8,128)(2,1)S(1)}, bf16[256,256]{1,0:T(8,128)(2,1)}, u32[]{:S(2)}) copy-start(bf16[256,256]{1,0:T(8,128)(2,1)} %constant.19.clone.block_table_ref) | copy-start | bytes 393220
  61.2 27.8 %all-to-all-start.1 = ((f32[64,16,128]{2,1,0:T(8,128)}), f32[64,16,128]{2,1,0:T(8,128)S(1)}, u32[]{:S(2)}, u32[]{:S(2)}) async-start(f32[64,16,128]{2,1,0:T(8,128)} %bitcast.6), calls=%async_computation.1 | async-start | bytes 1048576 | tf_op jit(solution)/shard_map/all_to_all | solution.py:179
  90.5 9.7 %collective-permute-start = (f32[128,512]{1,0:T(8,128)S(1)}, f32[128,512]{1,0:T(8,128)S(1)}, u32[]{:S(2)}, u32[]{:S(2)}) collective-permute-start(f32[128,512]{1,0:T(8,128)S(1)} %get-tuple-element.11), channel_id=1, source_target_pairs={{0,2},{1,3},{2,4},{3,5},{4,6},{5,7},{6,8},{7,9},{8,10},{9,11},{10,... | collective-permute-start | bytes 786440 | tf_op jit(solution)/shard_map/ppermute | solution.py:165
  92.5 13.9 %collective-permute-start.1 = (f32[128,512]{1,0:T(8,128)S(1)}, f32[128,512]{1,0:T(8,128)S(1)}, u32[]{:S(2)}, u32[]{:S(2)}) collective-permute-start(f32[128,512]{1,0:T(8,128)S(1)} %get-tuple-element.12), channel_id=1, source_target_pairs={{0,14},{1,15},{2,0},{3,1},{4,2},{5,3},{6,4},{7,5},{8,6},{9,7},{10,... | collective-permute-start | bytes 786440 | tf_op jit(solution)/shard_map/ppermute | solution.py:165
  96.3 13.1 %collective-permute-start.2 = (f32[128,512]{1,0:T(8,128)S(1)}, f32[128,512]{1,0:T(8,128)S(1)}, u32[]{:S(2)}, u32[]{:S(2)}) collective-permute-start(f32[128,512]{1,0:T(8,128)S(1)} %get-tuple-element.13), channel_id=1, source_target_pairs={{0,4},{1,13},{2,6},{3,15},{4,8},{5,1},{6,10},{7,3},{8,12},{9,5},{1... | collective-permute-start | bytes 786440 | tf_op jit(solution)/shard_map/ppermute | solution.py:165
  98.3 13.1 %collective-permute-start.3 = (f32[128,512]{1,0:T(8,128)S(1)}, f32[128,512]{1,0:T(8,128)S(1)}, u32[]{:S(2)}, u32[]{:S(2)}) collective-permute-start(f32[128,512]{1,0:T(8,128)S(1)} %get-tuple-element.10.refs_0_), channel_id=1, source_target_pairs={{0,1},{1,0},{2,3},{3,2},{4,5},{5,4},{6,7},{7,6},{8,9},{9,8},{10,11... | collective-permute-start | bytes 786440 | tf_op jit(solution)/shard_map/ppermute | solution.py:157
  100.2 11.2 %collective-permute-start.4 = (f32[128,512]{1,0:T(8,128)S(1)}, f32[128,512]{1,0:T(8,128)S(1)}, u32[]{:S(2)}, u32[]{:S(2)}) collective-permute-start(f32[128,512]{1,0:T(8,128)S(1)} %collective-permute-done.refs_1_), channel_id=1, source_target_pairs={{0,1},{1,0},{2,3},{3,2},{4,5},{5,4},{6,7},{7,6},{8,9},{9,8},{10,11... | collective-permute-start | bytes 786440 | tf_op jit(solution)/shard_map/ppermute | solution.py:157
  106.4 5.0 %collective-permute-start.5 = (f32[128,512]{1,0:T(8,128)S(1)}, f32[128,512]{1,0:T(8,128)S(1)}, u32[]{:S(2)}, u32[]{:S(2)}) collective-permute-start(f32[128,512]{1,0:T(8,128)S(1)} %collective-permute-done.1.refs_2_), channel_id=1, source_target_pairs={{0,1},{1,0},{2,3},{3,2},{4,5},{5,4},{6,7},{7,6},{8,9},{9,8},{10,11... | collective-permute-start | bytes 786440 | tf_op jit(solution)/shard_map/ppermute | solution.py:157
  109.5 3.4 %collective-permute-start.6 = (f32[128,512]{1,0:T(8,128)S(1)}, f32[128,512]{1,0:T(8,128)S(1)}, u32[]{:S(2)}, u32[]{:S(2)}) collective-permute-start(f32[128,512]{1,0:T(8,128)S(1)} %collective-permute-done.2.refs_3_), channel_id=1, source_target_pairs={{0,1},{1,0},{2,3},{3,2},{4,5},{5,4},{6,7},{7,6},{8,9},{9,8},{10,11... | collective-permute-start | bytes 786440 | tf_op jit(solution)/shard_map/ppermute | solution.py:157
  112.9 1.0 copy-start.2

commit v7 on v6

--- a/solution.py
+++ b/solution.py
@@ -98,11 +98,9 @@
     lax.fori_loop(0, GROUPS // 8, eight, 0)
 
 
-def order_kernel(y_high_ref, column_ref, got_ref, own_ref, up_ref, down_ref, far_ref, sketch_ref, other_ref):
-    column = column_ref[0]
-    ring = y_high_ref[0] * 4 + jnp.right_shift(column, 1)
-    far = 2 + 4 * jnp.bitwise_and(column, 1)
-    for step, target in ((0, own_ref), (1, up_ref), (7, down_ref), (far, far_ref)):
+def half_columns(y_high_ref, column_ref, got_ref, steps, targets):
+    ring = y_high_ref[0] * 4 + jnp.right_shift(column_ref[0], 1)
+    for step, target in zip(steps, targets):
         y_high = jnp.right_shift(jnp.bitwise_and(ring + step, 7), 2)
         for whose in range(2):
             for q in range(4):
@@ -110,25 +108,40 @@
                     place = jnp.bitwise_xor(y_high_ref[0], whose) * 8 + (y_high * (16 * 32) + q * 2 + part)
                     start = whose * 256 + part * 128
                     target[q * 32 : q * 32 + 32, start : start + 128] = got_ref[pl.ds(place, 32, stride=16), :]
-    for whose, target in enumerate((sketch_ref, other_ref)):
+
+
+def far_kernel(y_high_ref, column_ref, got_ref, far_ref):
+    step = 2 + 4 * jnp.bitwise_and(column_ref[0], 1)
+    half_columns(y_high_ref, column_ref, got_ref, (step,), (far_ref,))
+
+
+def order_kernel(y_high_ref, column_ref, got_ref, own_ref, up_ref, down_ref, sketch_ref, right_ref):
+    half_columns(y_high_ref, column_ref, got_ref, (0, 1, 7), (own_ref, up_ref, down_ref))
+    for whose in range(2):
+        columns = []
         for q in range(4):
             halves = [got_ref[pl.ds(whose * 8 + q * 2 + part, GROUPS, stride=16), :] for part in range(2)]
-            target[:, q * GROUPS : (q + 1) * GROUPS] = jnp.concatenate(halves, 1).T
-
-
-def gram_kernel(y_high_ref, column_ref, sketch_ref, other_ref, *refs):
-    parts, out_ref = refs[:-1], refs[-1]
+            columns.append(jnp.concatenate(halves, 1))
+        rows = jnp.concatenate(columns, 0).T
+        start = pl.multiple_of(jnp.bitwise_xor(y_high_ref[0], whose) * 256, 256)
+        right_ref[pl.ds(start, 256), :] = rows
+        if whose == 0:
+            sketch_ref[...] = rows
+
+
+CHIPS_ON = (0, 2, 3, 1)
+
+
+def gram_kernel(column_ref, right_ref, *refs):
+    out_ref = refs[-1]
+    parts = [ref.at[i : i + 128] for ref in refs[:-1] for i in range(0, ref.shape[0], 128)]
     chip = jnp.right_shift(column_ref[0], 1)
     core = jnp.bitwise_and(column_ref[0], 1)
-    first = y_high_ref[0] == 0
-    sketch, other = sketch_ref[...], other_ref[...]
-    right_high, right_low = split(
-        jnp.concatenate([jnp.where(first, sketch, other), jnp.where(first, other, sketch)], 0)
-    )
+    right_high, right_low = split(right_ref[...])
     for block, part in enumerate(parts):
         left_high, left_low = split(part[...])
         product = dot(left_high, right_high) + dot(left_high, right_low) + dot(left_low, right_high)
-        chip_of = jnp.bitwise_and(chip + (0, 3, 1, 2)[block % 4], 3)
+        chip_of = jnp.bitwise_and(chip + CHIPS_ON[block % 4], 3)
         core_of = jnp.bitwise_xor(core, block // 4)
         place = chip_of * 256 + core_of * 64
         for q in range(4):
@@ -182,21 +195,18 @@
     smem = pl.BlockSpec(memory_space=pltpu.SMEM)
     y_high = jnp.bitwise_and(lax.axis_index("row"), 1).astype(jnp.int32)[None]
     me = lax.axis_index("col").astype(jnp.int32)[None]
-    own, up, down, far, sketch, other = call(
+    places = [smem, smem, vmem]
+    far = call(far_kernel, shape(128, 512), in_specs=places)(y_high, me, picked)
+    far = around_ring(far, (2, 6))
+    own, up, down, sketch, right = call(
         order_kernel,
-        [shape(128, 512)] * 4 + [shape(256, 256)] * 2,
-        in_specs=[smem, smem, vmem],
+        [shape(128, 512)] * 3 + [shape(256, 256), shape(512, 256)],
+        in_specs=places,
     )(y_high, me, picked)
-    pieces = [
-        own,
-        around_ring(up, (1, 1)),
-        around_ring(down, (7, 7)),
-        around_ring(far, (2, 6)),
-    ]
-    pieces += [from_partner(piece, "col", 1) for piece in pieces]
-    gram = call(gram_kernel, shape(1024, 256), in_specs=[smem, smem] + [vmem] * 10)(
-        y_high, me, sketch, other, *pieces
-    )
+    sides = [around_ring(up, (1, 1)), around_ring(down, (7, 7))]
+    pieces = [own, far, *sides]
+    pieces += [from_partner(jnp.concatenate(pair, 0), "col", 1) for pair in ((own, far), sides)]
+    gram = call(gram_kernel, shape(1024, 256), in_specs=[smem] + [vmem] * 7)(me, right, *pieces)
 
     near = [[x * 16 + h * 4 + l * 2 + y for x in range(4) for l in range(2)] for h in range(4) for y in range(2)]
     far = [[x * 16 + h * 4 + l * 2 + y for h in range(4)] for x in range(4) for l in range(2) for y in range(2)]

time: 147 us -> 142 us (0.966)
  starting transfers between devices: 21.6 us -> 17.3 us
    ppermute x4 -> x2, starting transfers between devices: 8.12 us -> 3.84 us  [from_partner(): lax.ppermute(x, axis, [(i, i ^ distance) for i in range(lax.axis_size(axi...]
    unnamed x12 -> x10, local copies, waits for them, and re-layouts: 3.55 us -> 2.6 us
  transfers between devices with their start and end apart: 8 -> 6, of which waited for: 4 -> 4; matrix products, arithmetic and copies ran while one was open for 0% -> 0% of each run, Pallas kernels for 0% -> 1%
where the time goes in v7:
time: 142 us
  blocking collectives  84 us (59%)
  waiting for transfers between devices  29.4 us (21%)
  starting transfers between devices  17.3 us (12%)
  Pallas kernels  7.03 us (5%)
  local copies, waits for them, and re-layouts  2.6 us (2%)
    all_to_all x1, blocking collectives, shards(): lax.all_to_all(chunks.reshape(GROUPS, TILES, 2, 128), 'row', 0, 0, tiled=...  53.2 us
    all_to_all x1, waiting for transfers between devices, shards(): lax.all_to_all(picked, 'row', 0, 0, tiled=True).reshape(16 * GROUPS, 128)  22.1 us
    all_to_all x1, blocking collectives, shards(): gram = lax.all_to_all(gram, 'row', 0, 0, axis_index_groups=near, tiled=True)  19.3 us
    all_to_all x1, blocking collectives, shards(): gram = lax.all_to_all(gram, 'row', 0, 0, axis_index_groups=far, tiled=True)  11.5 us
    ppermute x3, starting transfers between devices, around_ring(): return lax.ppermute(x, ('row', 'col'), pairs)  7.75 us
    all_to_all x1, starting transfers between devices, shards(): lax.all_to_all(picked, 'row', 0, 0, tiled=True).reshape(16 * GROUPS, 128)  5.7 us
    ppermute x3, waiting for transfers between devices, around_ring(): return lax.ppermute(x, ('row', 'col'), pairs)  5.42 us
    pallas_call x1, Pallas kernels, shards(): call(mix_kernel, shape(16 * GROUPS, 128), [pltpu.VMEM((8 * GROUPS, 128),...  4.08 us
  transfers between devices with their start and end apart: 6, of which 4 were waited for; matrix products, arithmetic and copies ran while one was open for 0% of the time, Pallas kernels for 1%

profile of v7, /device:TPU:8, one launch (start us, length us, event | category | flops | bytes accessed | tf_op | source)
XLA Modules:
  0.0 141.8 jit_solution(14173171212807135674)
XLA Ops:
  0.6 1.2 copy-done
  1.9 0.7 copy-done.3
  2.5 0.7 copy-done.4
  3.2 0.7 shard_map.68
  3.9 0.0 copy-start.1
  4.0 53.2 %all_to_all.28 = f32[64,17,2,128]{3,2,1,0:T(2,128)S(1)} all-to-all(f32[64,17,2,128]{3,2,1,0:T(2,128)S(1)} %bitcast.13), channel_id=1, replica_groups=mesh['row'=64,'col'=8] {'row'}, dimensions={0} | all-to-all | bytes 2228224 | tf_op jit(solution)/shard_map/all_to_all | solution.py:185
  57.1 4.1 %shard_map.69 = f32[1024,128]{1,0:T(8,128)} custom-call(f32[1088,2,128]{2,1,0:T(2,128)S(1)} %bitcast.12, bf16[256,256]{1,0:T(8,128)(2,1)S(1)} %copy-done.2, bf16[512,512]{1,0:T(8,128)(2,1)S(1)} %copy-done.1), custom_call_target="tpu_custom_call" | custom-call | tf_op jit(solution)/shard_map/pallas_call | solution.py:188
  61.2 5.7 %all-to-all-start.1 = ((f32[64,16,128]{2,1,0:T(8,128)}), f32[64,16,128]{2,1,0:T(8,128)S(1)}, u32[]{:S(2)}, u32[]{:S(2)}) async-start(f32[64,16,128]{2,1,0:T(8,128)} %bitcast.6), calls=%async_computation.1 | async-start | bytes 1048576 | tf_op jit(solution)/shard_map/all_to_all | solution.py:192
  66.9 22.1 %all-to-all-done.1 = f32[64,16,128]{2,1,0:T(8,128)S(1)} async-done(((f32[64,16,128]{2,1,0:T(8,128)}), f32[64,16,128]{2,1,0:T(8,128)S(1)}, u32[]{:S(2)}, u32[]{:S(2)}) %all-to-all-start.1) | async-done | bytes 524320 | tf_op jit(solution)/shard_map/all_to_all | solution.py:192
  89.0 0.1 shard_map.71
  89.1 1.9 %collective-permute-start = (f32[128,512]{1,0:T(8,128)S(1)}, f32[128,512]{1,0:T(8,128)S(1)}, u32[]{:S(2)}, u32[]{:S(2)}) collective-permute-start(f32[128,512]{1,0:T(8,128)S(1)} %shard_map.71), channel_id=1, source_target_pairs={{0,4},{1,13},{2,6},{3,15},{4,8},{5,1},{6,10},{7,3},{8,12},{9,5},{1... | collective-permute-start | bytes 786440 | tf_op jit(solution)/shard_map/ppermute | solution.py:178
  91.1 1.1 shard_map.70
  92.2 2.0 %collective-permute-start.1 = (f32[128,512]{1,0:T(8,128)S(1)}, f32[128,512]{1,0:T(8,128)S(1)}, u32[]{:S(2)}, u32[]{:S(2)}) collective-permute-start(f32[128,512]{1,0:T(8,128)S(1)} %get-tuple-element.10), channel_id=1, source_target_pairs={{0,2},{1,3},{2,4},{3,5},{4,6},{5,7},{6,8},{7,9},{8,10},{9,11},{10,... | collective-permute-start | bytes 786440 | tf_op jit(solution)/shard_map/ppermute | solution.py:178
  94.2 3.8 %collective-permute-start.2 = (f32[128,512]{1,0:T(8,128)S(1)}, f32[128,512]{1,0:T(8,128)S(1)}, u32[]{:S(2)}, u32[]{:S(2)}) collective-permute-start(f32[128,512]{1,0:T(8,128)S(1)} %get-tuple-element.11), channel_id=1, source_target_pairs={{0,14},{1,15},{2,0},{3,1},{4,2},{5,3},{6,4},{7,5},{8,6},{9,7},{10,... | collective-permute-start | bytes 786440 | tf_op jit(solution)/shard_map/ppermute | solution.py:178
  98.0 4.5 %collective-permute-done.refs_1_ = f32[128,512]{1,0:T(8,128)S(1)} collective-permute-done((f32[128,512]{1,0:T(8,128)S(1)}, f32[128,512]{1,0:T(8,128)S(1)}, u32[]{:S(2)}, u32[]{:S(2)}) %collective-permute-start) | collective-permute-done | bytes 262176 | tf_op jit(solution)/shard_map/ppermute | solution.py:178
  102.5 1.9 %collective-permute-start.3 = (f32[256,512]{1,0:T(8,128)S(1)}, f32[256,512]{1,0:T(8,128)S(1)}, u32[]{:S(2)}, u32[]{:S(2)}) collective-permute-start(f32[256,512]{1,0:T(8,128)S(1)} %pad_maximum_fusion), channel_id=1, source_target_pairs={{0,1},{1,0},{2,3},{3,2},{4,5},{5,4},{6,7},{7,6},{8,9},{9,8},{10,11... | collective-permute-start | bytes 1572872 | tf_op jit(solution)/shard_map/ppermute | solution.py:170
  104.4 0.9 collective-permute-done.1.refs_2_
  105.4 1.9 %collective-permute-start.4 = (f32[256,512]{1,0:T(8,128)S(1)}, f32[256,512]{1,0:T(8,128)S(1)}, u32[]{:S(2)}, u32[]{:S(2)}) collective-permute-start(f32[256,512]{1,0:T(8,128)S(1)} %pad_maximum_fusion.1), channel_id=1, source_target_pairs={{0,1},{1,0},{2,3},{3,2},{4,5},{5,4},{6,7},{7,6},{8,9},{9,8},{10,11... | collective-permute-start | bytes 1572872 | tf_op jit(solution)/shard_map/ppermute | solution.py:170
  107.4 1.9 %collective-permute-done.4.refs_5_ = f32[256,512]{1,0:T(8,128)S(1)} collective-permute-done((f32[256,512]{1,0:T(8,128)S(1)}, f32[256,512]{1,0:T(8,128)S(1)}, u32[]{:S(2)}, u32[]{:S(2)}) %collective-permute-start.4) | collective-permute-done | bytes 524320 | tf_op jit(solution)/shard_map/ppermute | solution.py:170
  109.2 1.1 shard_map.72
  110.3 19.3 %all_to_all.29 = f32[8,128,256]{2,1,0:T(8,128)S(1)} all-to-all(f32[8,128,256]{2,1,0:T(8,128)S(1)} %bitcast.14), channel_id=1, replica_groups={{0,16,128,144,256,272,384,400},{8,24,136,152,264,280,392,408},{32,48,16..., dimensions={0} | all-to-all | bytes 2097152 | tf_op jit(solution)/shard_map/all_to_all | solution.py:213
  129.6 0.1 reduce_sum.18
  129.7 11.5 %all_to_all.30 = f32[4,32,256]{2,1,0:T(8,128)S(1)} all-to-all(f32[4,32,256]{2,1,0:T(8,128)S(1)} %bitcast.17), channel_id=1, replica_groups={{0,32,64,96},{8,40,72,104},{16,48,80,112},{24,56,88,120},{128,160,192,2..., dimensions={0} | all-to-all | bytes 262144 | tf_op jit(solution)/shard_map/all_to_all | solution.py:215
  141.2 0.6 broadcast_multiply_fusion
  (11 shorter events, 0.1 us)
Async XLA Ops:
  0.6 1.2 copy-start
  1.9 0.7 copy-start.3
  2.5 0.7 copy-start.4
  3.9 53.2 %copy-start.1 = (bf16[512,512]{1,0:T(8,128)(2,1)S(1)}, bf16[512,512]{1,0:T(8,128)(2,1)}, u32[]{:S(2)}) copy-start(bf16[512,512]{1,0:T(8,128)(2,1)} %constant.20.clone.lane_table_ref) | copy-start | bytes 1572868
  3.9 53.2 %copy-start.2 = (bf16[256,256]{1,0:T(8,128)(2,1)S(1)}, bf16[256,256]{1,0:T(8,128)(2,1)}, u32[]{:S(2)}) copy-start(bf16[256,256]{1,0:T(8,128)(2,1)} %constant.19.clone.block_table_ref) | copy-start | bytes 393220
  61.2 27.8 %all-to-all-start.1 = ((f32[64,16,128]{2,1,0:T(8,128)}), f32[64,16,128]{2,1,0:T(8,128)S(1)}, u32[]{:S(2)}, u32[]{:S(2)}) async-start(f32[64,16,128]{2,1,0:T(8,128)} %bitcast.6), calls=%async_computation.1 | async-start | bytes 1048576 | tf_op jit(solution)/shard_map/all_to_all | solution.py:192
  89.1 13.4 %collective-permute-start = (f32[128,512]{1,0:T(8,128)S(1)}, f32[128,512]{1,0:T(8,128)S(1)}, u32[]{:S(2)}, u32[]{:S(2)}) collective-permute-start(f32[128,512]{1,0:T(8,128)S(1)} %shard_map.71), channel_id=1, source_target_pairs={{0,4},{1,13},{2,6},{3,15},{4,8},{5,1},{6,10},{7,3},{8,12},{9,5},{1... | collective-permute-start | bytes 786440 | tf_op jit(solution)/shard_map/ppermute | solution.py:178
  92.2 13.2 %collective-permute-start.1 = (f32[128,512]{1,0:T(8,128)S(1)}, f32[128,512]{1,0:T(8,128)S(1)}, u32[]{:S(2)}, u32[]{:S(2)}) collective-permute-start(f32[128,512]{1,0:T(8,128)S(1)} %get-tuple-element.10), channel_id=1, source_target_pairs={{0,2},{1,3},{2,4},{3,5},{4,6},{5,7},{6,8},{7,9},{8,10},{9,11},{10,... | collective-permute-start | bytes 786440 | tf_op jit(solution)/shard_map/ppermute | solution.py:178
  94.2 11.2 %collective-permute-start.2 = (f32[128,512]{1,0:T(8,128)S(1)}, f32[128,512]{1,0:T(8,128)S(1)}, u32[]{:S(2)}, u32[]{:S(2)}) collective-permute-start(f32[128,512]{1,0:T(8,128)S(1)} %get-tuple-element.11), channel_id=1, source_target_pairs={{0,14},{1,15},{2,0},{3,1},{4,2},{5,3},{6,4},{7,5},{8,6},{9,7},{10,... | collective-permute-start | bytes 786440 | tf_op jit(solution)/shard_map/ppermute | solution.py:178
  102.5 4.8 %collective-permute-start.3 = (f32[256,512]{1,0:T(8,128)S(1)}, f32[256,512]{1,0:T(8,128)S(1)}, u32[]{:S(2)}, u32[]{:S(2)}) collective-permute-start(f32[256,512]{1,0:T(8,128)S(1)} %pad_maximum_fusion), channel_id=1, source_target_pairs={{0,1},{1,0},{2,3},{3,2},{4,5},{5,4},{6,7},{7,6},{8,9},{9,8},{10,11... | collective-permute-start | bytes 1572872 | tf_op jit(solution)/shard_map/ppermute | solution.py:170
  105.4 3.8 %collective-permute-start.4 = (f32[256,512]{1,0:T(8,128)S(1)}, f32[256,512]{1,0:T(8,128)S(1)}, u32[]{:S(2)}, u32[]{:S(2)}) collective-permute-start(f32[256,512]{1,0:T(8,128)S(1)} %pad_maximum_fusion.1), channel_id=1, source_target_pairs={{0,1},{1,0},{2,3},{3,2},{4,5},{5,4},{6,7},{7,6},{8,9},{9,8},{10,11... | collective-permute-start | bytes 1572872 | tf_op jit(solution)/shard_map/ppermute | solution.py:170

commit v8 on v7

--- a/solution.py
+++ b/solution.py
@@ -91,11 +91,12 @@
                 jnp.where(up_b, b, pltpu.roll(b, 1, 0)),
             )
             partner = group * 8 + (inner ^ 1)
-            out_ref[pl.ds(pl.multiple_of(block * 16, 8), 8), :] = picked
-            out_ref[pl.ds(pl.multiple_of(partner * 16 + 8, 8), 8), :] = picked
+            out_ref[pl.ds(block * 16, 8), :] = picked
+            out_ref[pl.ds(partner * 16 + 8, 8), :] = picked
         return carry
 
-    lax.fori_loop(0, GROUPS // 8, eight, 0)
+    for group in range(GROUPS // 8):
+        eight(group, 0)
 
 
 def half_columns(y_high_ref, column_ref, got_ref, steps, targets):
@@ -115,8 +116,11 @@
     half_columns(y_high_ref, column_ref, got_ref, (step,), (far_ref,))
 
 
-def order_kernel(y_high_ref, column_ref, got_ref, own_ref, up_ref, down_ref, sketch_ref, right_ref):
+def near_kernel(y_high_ref, column_ref, got_ref, own_ref, up_ref, down_ref):
     half_columns(y_high_ref, column_ref, got_ref, (0, 1, 7), (own_ref, up_ref, down_ref))
+
+
+def order_kernel(y_high_ref, got_ref, sketch_ref, right_ref):
     for whose in range(2):
         columns = []
         for q in range(4):
@@ -146,7 +150,7 @@
         place = chip_of * 256 + core_of * 64
         for q in range(4):
             start = pl.multiple_of(place + (q % 2) * 128 + (q // 2) * 32, 32)
-            out_ref[pl.ds(start, 32), :] = product[q * 32 : q * 32 + 32]
+            out_ref[pl.ds(start, 32), :] = product[q * 32 : q * 32 + 32] * F32(2.0**-14)
 
 
 def call(kernel, out_shape, scratch=(), **more):
@@ -198,11 +202,10 @@
     places = [smem, smem, vmem]
     far = call(far_kernel, shape(128, 512), in_specs=places)(y_high, me, picked)
     far = around_ring(far, (2, 6))
-    own, up, down, sketch, right = call(
-        order_kernel,
-        [shape(128, 512)] * 3 + [shape(256, 256), shape(512, 256)],
-        in_specs=places,
-    )(y_high, me, picked)
+    own, up, down = call(near_kernel, [shape(128, 512)] * 3, in_specs=places)(y_high, me, picked)
+    sketch, right = call(order_kernel, [shape(256, 256), shape(512, 256)], in_specs=[smem, vmem])(
+        y_high, picked
+    )
     sides = [around_ring(up, (1, 1)), around_ring(down, (7, 7))]
     pieces = [own, far, *sides]
     pieces += [from_partner(jnp.concatenate(pair, 0), "col", 1) for pair in ((own, far), sides)]
@@ -213,7 +216,7 @@
     gram = lax.all_to_all(gram, "row", 0, 0, axis_index_groups=near, tiled=True)
     gram = jnp.sum(gram.reshape(8, 128, 256), 0)
     gram = lax.all_to_all(gram, "row", 0, 0, axis_index_groups=far, tiled=True)
-    gram = jnp.sum(gram.reshape(4, 32, 256), 0) * F32(2.0**-14)
+    gram = jnp.sum(gram.reshape(4, 32, 256), 0)
     return sketch, gram
 
 

time: 142 us -> 142 us (level)
  no operation moved by 1% of the time
where the time goes in v8:
time: 142 us; the launch traced here: 141 us
  blocking collectives  84 us (59%)
  waiting for transfers between devices  29.4 us (21%)
  starting transfers between devices  17.3 us (12%)
  Pallas kernels  6.62 us (5%)
  local copies, waits for them, and re-layouts  2.6 us (2%)
    all_to_all x1, blocking collectives, shards(): lax.all_to_all(chunks.reshape(GROUPS, TILES, 2, 128), 'row', 0, 0, tiled=...  53.2 us
    all_to_all x1, waiting for transfers between devices, shards(): lax.all_to_all(picked, 'row', 0, 0, tiled=True).reshape(16 * GROUPS, 128)  22.1 us
    all_to_all x1, blocking collectives, shards(): gram = lax.all_to_all(gram, 'row', 0, 0, axis_index_groups=near, tiled=True)  19.3 us
    all_to_all x1, blocking collectives, shards(): gram = lax.all_to_all(gram, 'row', 0, 0, axis_index_groups=far, tiled=True)  11.5 us
    ppermute x3, starting transfers between devices, around_ring(): return lax.ppermute(x, ('row', 'col'), pairs)  7.76 us
    ppermute x3, waiting for transfers between devices, around_ring(): return lax.ppermute(x, ('row', 'col'), pairs)  6.25 us
    all_to_all x1, starting transfers between devices, shards(): lax.all_to_all(picked, 'row', 0, 0, tiled=True).reshape(16 * GROUPS, 128)  5.69 us
    ppermute x2, starting transfers between devices, from_partner(): lax.ppermute(x, axis, [(i, i ^ distance) for i in range(lax.axis_size(axi...  3.84 us
  transfers between devices with their start and end apart: 6, of which 4 were waited for; matrix products, arithmetic and copies ran while one was open for 0% of the time, Pallas kernels for 1%

profile of v8, /device:TPU:8, one launch (start us, length us, event | category | flops | bytes accessed | tf_op | source)
XLA Modules:
  0.0 141.4 jit_solution(13928975468293207226)
XLA Ops:
  0.6 1.2 copy-done
  1.9 0.7 copy-done.3
  2.5 0.7 copy-done.4
  3.2 0.7 shard_map.68
  4.0 53.2 %all_to_all.28 = f32[64,17,2,128]{3,2,1,0:T(2,128)S(1)} all-to-all(f32[64,17,2,128]{3,2,1,0:T(2,128)S(1)} %bitcast.14), channel_id=1, replica_groups=mesh['row'=64,'col'=8] {'row'}, dimensions={0} | all-to-all | bytes 2228224 | tf_op jit(solution)/shard_map/all_to_all | solution.py:189
  57.1 3.7 %shard_map.69 = f32[1024,128]{1,0:T(8,128)} custom-call(f32[1088,2,128]{2,1,0:T(2,128)S(1)} %bitcast.13, bf16[256,256]{1,0:T(8,128)(2,1)S(1)} %copy-done.2, bf16[512,512]{1,0:T(8,128)(2,1)S(1)} %copy-done.1), custom_call_target="tpu_custom_call" | custom-call | tf_op jit(solution)/shard_map/pallas_call | solution.py:192
  60.8 5.7 %all-to-all-start.1 = ((f32[64,16,128]{2,1,0:T(8,128)}), f32[64,16,128]{2,1,0:T(8,128)S(1)}, u32[]{:S(2)}, u32[]{:S(2)}) async-start(f32[64,16,128]{2,1,0:T(8,128)} %bitcast.5), calls=%async_computation.1 | async-start | bytes 1048576 | tf_op jit(solution)/shard_map/all_to_all | solution.py:196
  66.5 22.1 %all-to-all-done.1 = f32[64,16,128]{2,1,0:T(8,128)S(1)} async-done(((f32[64,16,128]{2,1,0:T(8,128)}), f32[64,16,128]{2,1,0:T(8,128)S(1)}, u32[]{:S(2)}, u32[]{:S(2)}) %all-to-all-start.1) | async-done | bytes 524320 | tf_op jit(solution)/shard_map/all_to_all | solution.py:196
  88.6 0.1 shard_map.72
  88.7 1.9 %collective-permute-start = (f32[128,512]{1,0:T(8,128)S(1)}, f32[128,512]{1,0:T(8,128)S(1)}, u32[]{:S(2)}, u32[]{:S(2)}) collective-permute-start(f32[128,512]{1,0:T(8,128)S(1)} %shard_map.72), channel_id=1, source_target_pairs={{0,4},{1,13},{2,6},{3,15},{4,8},{5,1},{6,10},{7,3},{8,12},{9,5},{1... | collective-permute-start | bytes 786440 | tf_op jit(solution)/shard_map/ppermute | solution.py:182
  90.6 0.3 shard_map.71
  90.9 2.0 %collective-permute-start.1 = (f32[128,512]{1,0:T(8,128)S(1)}, f32[128,512]{1,0:T(8,128)S(1)}, u32[]{:S(2)}, u32[]{:S(2)}) collective-permute-start(f32[128,512]{1,0:T(8,128)S(1)} %get-tuple-element.10), channel_id=1, source_target_pairs={{0,2},{1,3},{2,4},{3,5},{4,6},{5,7},{6,8},{7,9},{8,10},{9,11},{10,... | collective-permute-start | bytes 786440 | tf_op jit(solution)/shard_map/ppermute | solution.py:182
  92.9 3.8 %collective-permute-start.2 = (f32[128,512]{1,0:T(8,128)S(1)}, f32[128,512]{1,0:T(8,128)S(1)}, u32[]{:S(2)}, u32[]{:S(2)}) collective-permute-start(f32[128,512]{1,0:T(8,128)S(1)} %get-tuple-element.11), channel_id=1, source_target_pairs={{0,14},{1,15},{2,0},{3,1},{4,2},{5,3},{6,4},{7,5},{8,6},{9,7},{10,... | collective-permute-start | bytes 786440 | tf_op jit(solution)/shard_map/ppermute | solution.py:182
  96.8 5.1 %collective-permute-done.refs_1_ = f32[128,512]{1,0:T(8,128)S(1)} collective-permute-done((f32[128,512]{1,0:T(8,128)S(1)}, f32[128,512]{1,0:T(8,128)S(1)}, u32[]{:S(2)}, u32[]{:S(2)}) %collective-permute-start) | collective-permute-done | bytes 262176 | tf_op jit(solution)/shard_map/ppermute | solution.py:182
  101.9 1.9 %collective-permute-start.3 = (f32[256,512]{1,0:T(8,128)S(1)}, f32[256,512]{1,0:T(8,128)S(1)}, u32[]{:S(2)}, u32[]{:S(2)}) collective-permute-start(f32[256,512]{1,0:T(8,128)S(1)} %pad_maximum_fusion), channel_id=1, source_target_pairs={{0,1},{1,0},{2,3},{3,2},{4,5},{5,4},{6,7},{7,6},{8,9},{9,8},{10,11... | collective-permute-start | bytes 1572872 | tf_op jit(solution)/shard_map/ppermute | solution.py:174
  103.8 1.1 collective-permute-done.1.refs_2_
  105.0 1.9 %collective-permute-start.4 = (f32[256,512]{1,0:T(8,128)S(1)}, f32[256,512]{1,0:T(8,128)S(1)}, u32[]{:S(2)}, u32[]{:S(2)}) collective-permute-start(f32[256,512]{1,0:T(8,128)S(1)} %pad_maximum_fusion.1), channel_id=1, source_target_pairs={{0,1},{1,0},{2,3},{3,2},{4,5},{5,4},{6,7},{7,6},{8,9},{9,8},{10,11... | collective-permute-start | bytes 1572872 | tf_op jit(solution)/shard_map/ppermute | solution.py:174
  106.9 0.9 shard_map.70
  107.8 1.0 collective-permute-done.4.refs_5_
  108.8 1.1 shard_map.73
  109.9 19.3 %all_to_all.29 = f32[8,128,256]{2,1,0:T(8,128)S(1)} all-to-all(f32[8,128,256]{2,1,0:T(8,128)S(1)} %bitcast.15), channel_id=1, replica_groups={{0,16,128,144,256,272,384,400},{8,24,136,152,264,280,392,408},{32,48,16..., dimensions={0} | all-to-all | bytes 2097152 | tf_op jit(solution)/shard_map/all_to_all | solution.py:216
  129.2 0.1 reduce_sum.18
  129.3 11.5 %all_to_all.30 = f32[4,32,256]{2,1,0:T(8,128)S(1)} all-to-all(f32[4,32,256]{2,1,0:T(8,128)S(1)} %bitcast.18), channel_id=1, replica_groups={{0,32,64,96},{8,40,72,104},{16,48,80,112},{24,56,88,120},{128,160,192,2..., dimensions={0} | all-to-all | bytes 262144 | tf_op jit(solution)/shard_map/all_to_all | solution.py:218
  140.7 0.6 reduce_sum.19
  (11 shorter events, 0.1 us)
Async XLA Ops:
  0.6 1.2 copy-start
  1.9 0.7 copy-start.3
  2.5 0.7 copy-start.4
  3.9 53.2 %copy-start.1 = (bf16[512,512]{1,0:T(8,128)(2,1)S(1)}, bf16[512,512]{1,0:T(8,128)(2,1)}, u32[]{:S(2)}) copy-start(bf16[512,512]{1,0:T(8,128)(2,1)} %constant.18.clone.lane_table_ref) | copy-start | bytes 1572868
  3.9 53.2 %copy-start.2 = (bf16[256,256]{1,0:T(8,128)(2,1)S(1)}, bf16[256,256]{1,0:T(8,128)(2,1)}, u32[]{:S(2)}) copy-start(bf16[256,256]{1,0:T(8,128)(2,1)} %constant.17.clone.block_table_ref) | copy-start | bytes 393220
  60.8 27.8 %all-to-all-start.1 = ((f32[64,16,128]{2,1,0:T(8,128)}), f32[64,16,128]{2,1,0:T(8,128)S(1)}, u32[]{:S(2)}, u32[]{:S(2)}) async-start(f32[64,16,128]{2,1,0:T(8,128)} %bitcast.5), calls=%async_computation.1 | async-start | bytes 1048576 | tf_op jit(solution)/shard_map/all_to_all | solution.py:196
  88.7 13.2 %collective-permute-start = (f32[128,512]{1,0:T(8,128)S(1)}, f32[128,512]{1,0:T(8,128)S(1)}, u32[]{:S(2)}, u32[]{:S(2)}) collective-permute-start(f32[128,512]{1,0:T(8,128)S(1)} %shard_map.72), channel_id=1, source_target_pairs={{0,4},{1,13},{2,6},{3,15},{4,8},{5,1},{6,10},{7,3},{8,12},{9,5},{1... | collective-permute-start | bytes 786440 | tf_op jit(solution)/shard_map/ppermute | solution.py:182
  90.9 14.1 %collective-permute-start.1 = (f32[128,512]{1,0:T(8,128)S(1)}, f32[128,512]{1,0:T(8,128)S(1)}, u32[]{:S(2)}, u32[]{:S(2)}) collective-permute-start(f32[128,512]{1,0:T(8,128)S(1)} %get-tuple-element.10), channel_id=1, source_target_pairs={{0,2},{1,3},{2,4},{3,5},{4,6},{5,7},{6,8},{7,9},{8,10},{9,11},{10,... | collective-permute-start | bytes 786440 | tf_op jit(solution)/shard_map/ppermute | solution.py:182
  92.9 12.1 %collective-permute-start.2 = (f32[128,512]{1,0:T(8,128)S(1)}, f32[128,512]{1,0:T(8,128)S(1)}, u32[]{:S(2)}, u32[]{:S(2)}) collective-permute-start(f32[128,512]{1,0:T(8,128)S(1)} %get-tuple-element.11), channel_id=1, source_target_pairs={{0,14},{1,15},{2,0},{3,1},{4,2},{5,3},{6,4},{7,5},{8,6},{9,7},{10,... | collective-permute-start | bytes 786440 | tf_op jit(solution)/shard_map/ppermute | solution.py:182
  101.9 5.9 %collective-permute-start.3 = (f32[256,512]{1,0:T(8,128)S(1)}, f32[256,512]{1,0:T(8,128)S(1)}, u32[]{:S(2)}, u32[]{:S(2)}) collective-permute-start(f32[256,512]{1,0:T(8,128)S(1)} %pad_maximum_fusion), channel_id=1, source_target_pairs={{0,1},{1,0},{2,3},{3,2},{4,5},{5,4},{6,7},{7,6},{8,9},{9,8},{10,11... | collective-permute-start | bytes 1572872 | tf_op jit(solution)/shard_map/ppermute | solution.py:174
  105.0 3.8 %collective-permute-start.4 = (f32[256,512]{1,0:T(8,128)S(1)}, f32[256,512]{1,0:T(8,128)S(1)}, u32[]{:S(2)}, u32[]{:S(2)}) collective-permute-start(f32[256,512]{1,0:T(8,128)S(1)} %pad_maximum_fusion.1), channel_id=1, source_target_pairs={{0,1},{1,0},{2,3},{3,2},{4,5},{5,4},{6,7},{7,6},{8,9},{9,8},{10,11... | collective-permute-start | bytes 1572872 | tf_op jit(solution)/shard_map/ppermute | solution.py:174

commit v9 on v8

--- a/solution.py
+++ b/solution.py
@@ -116,41 +116,48 @@
     half_columns(y_high_ref, column_ref, got_ref, (step,), (far_ref,))
 
 
-def near_kernel(y_high_ref, column_ref, got_ref, own_ref, up_ref, down_ref):
+def near_kernel(y_high_ref, column_ref, got_ref, after_ref, own_ref, up_ref, down_ref):
     half_columns(y_high_ref, column_ref, got_ref, (0, 1, 7), (own_ref, up_ref, down_ref))
 
 
-def order_kernel(y_high_ref, got_ref, sketch_ref, right_ref):
+def order_kernel(y_high_ref, got_ref, after_ref, sketch_ref, right_ref, right_too_ref):
+    rows = []
     for whose in range(2):
         columns = []
         for q in range(4):
             halves = [got_ref[pl.ds(whose * 8 + q * 2 + part, GROUPS, stride=16), :] for part in range(2)]
             columns.append(jnp.concatenate(halves, 1))
-        rows = jnp.concatenate(columns, 0).T
-        start = pl.multiple_of(jnp.bitwise_xor(y_high_ref[0], whose) * 256, 256)
-        right_ref[pl.ds(start, 256), :] = rows
-        if whose == 0:
-            sketch_ref[...] = rows
-
-
-CHIPS_ON = (0, 2, 3, 1)
-
-
-def gram_kernel(column_ref, right_ref, *refs):
-    out_ref = refs[-1]
-    parts = [ref.at[i : i + 128] for ref in refs[:-1] for i in range(0, ref.shape[0], 128)]
+        rows.append(jnp.concatenate(columns, 0).T)
+    sketch_ref[...] = rows[0]
+    first = y_high_ref[0] == 0
+    right_ref[...] = jnp.where(first, rows[0], rows[1])
+    right_too_ref[...] = jnp.where(first, rows[1], rows[0])
+
+
+def products(lefts, rights):
+    right_high, right_low = split(jnp.concatenate([right[...] for right in rights], 0))
+    for block, left in enumerate(lefts):
+        left_high, left_low = split(left[...])
+        product = dot(left_high, right_high) + dot(left_high, right_low) + dot(left_low, right_high)
+        yield block, product * F32(2.0**-14)
+
+
+def half_gram_kernel(own_ref, far_ref, up_ref, down_ref, right_ref, right_too_ref, out_ref):
+    for block, product in products((own_ref, far_ref, up_ref, down_ref), (right_ref, right_too_ref)):
+        out_ref[block * 128 : block * 128 + 128, :] = product
+
+
+def gram_kernel(column_ref, half_ref, own_ref, far_ref, up_ref, down_ref, right_ref, right_too_ref, out_ref):
     chip = jnp.right_shift(column_ref[0], 1)
     core = jnp.bitwise_and(column_ref[0], 1)
-    right_high, right_low = split(right_ref[...])
-    for block, part in enumerate(parts):
-        left_high, left_low = split(part[...])
-        product = dot(left_high, right_high) + dot(left_high, right_low) + dot(left_low, right_high)
-        chip_of = jnp.bitwise_and(chip + CHIPS_ON[block % 4], 3)
-        core_of = jnp.bitwise_xor(core, block // 4)
-        place = chip_of * 256 + core_of * 64
+    for block, product in products((own_ref, far_ref, up_ref, down_ref), (right_ref, right_too_ref)):
+        place = jnp.bitwise_and(chip + (0, 2, 3, 1)[block], 3) * 256
         for q in range(4):
-            start = pl.multiple_of(place + (q % 2) * 128 + (q // 2) * 32, 32)
-            out_ref[pl.ds(start, 32), :] = product[q * 32 : q * 32 + 32] * F32(2.0**-14)
+            start = place + (q % 2) * 128 + (q // 2) * 32
+            mine = pl.multiple_of(start + core * 64, 32)
+            out_ref[pl.ds(mine, 32), :] = half_ref[block * 128 + q * 32 : block * 128 + q * 32 + 32, :]
+            others = pl.multiple_of(start + (1 - core) * 64, 32)
+            out_ref[pl.ds(others, 32), :] = product[q * 32 : q * 32 + 32]
 
 
 def call(kernel, out_shape, scratch=(), **more):
@@ -200,21 +207,35 @@
     y_high = jnp.bitwise_and(lax.axis_index("row"), 1).astype(jnp.int32)[None]
     me = lax.axis_index("col").astype(jnp.int32)[None]
     places = [smem, smem, vmem]
-    far = call(far_kernel, shape(128, 512), in_specs=places)(y_high, me, picked)
-    far = around_ring(far, (2, 6))
-    own, up, down = call(near_kernel, [shape(128, 512)] * 3, in_specs=places)(y_high, me, picked)
-    sketch, right = call(order_kernel, [shape(256, 256), shape(512, 256)], in_specs=[smem, vmem])(
-        y_high, picked
-    )
-    sides = [around_ring(up, (1, 1)), around_ring(down, (7, 7))]
-    pieces = [own, far, *sides]
-    pieces += [from_partner(jnp.concatenate(pair, 0), "col", 1) for pair in ((own, far), sides)]
-    gram = call(gram_kernel, shape(1024, 256), in_specs=[smem] + [vmem] * 7)(me, right, *pieces)
-
-    near = [[x * 16 + h * 4 + l * 2 + y for x in range(4) for l in range(2)] for h in range(4) for y in range(2)]
+    after = pl.BlockSpec(memory_space=pl.ANY)
+    far_left = call(far_kernel, shape(128, 512), in_specs=places)(y_high, me, picked)
+    far = around_ring(far_left, (2, 6))
+    own, up, down = call(near_kernel, [shape(128, 512)] * 3, in_specs=[*places, after])(
+        y_high, me, picked, far_left
+    )
+    sketch, *right = call(
+        order_kernel, [shape(256, 256)] * 3, in_specs=[smem, vmem, after]
+    )(y_high, picked, own)
+    up, down = around_ring(up, (1, 1)), around_ring(down, (7, 7))
+    other = [from_partner(part, "col", 1) for part in right]
+    half = call(
+        half_gram_kernel,
+        shape(512, 256),
+        cost_estimate=pl.CostEstimate(flops=6 * 512 * 512 * 256, bytes_accessed=2 << 20, transcendentals=0),
+    )(own, far, up, down, *right)
+    gram = call(gram_kernel, shape(1024, 256), in_specs=[smem] + [vmem] * 7)(
+        me, half, own, far, up, down, *other
+    )
+
+    near = [
+        [(x * 16 + h * 4 + l * 2 + y) * 8 + c * 2 + core for x in range(4) for l in range(2) for core in range(2)]
+        for h in range(4)
+        for y in range(2)
+        for c in range(4)
+    ]
     far = [[x * 16 + h * 4 + l * 2 + y for h in range(4)] for x in range(4) for l in range(2) for y in range(2)]
-    gram = lax.all_to_all(gram, "row", 0, 0, axis_index_groups=near, tiled=True)
-    gram = jnp.sum(gram.reshape(8, 128, 256), 0)
+    gram = lax.all_to_all(gram, ("row", "col"), 0, 0, axis_index_groups=near, tiled=True)
+    gram = jnp.sum(gram.reshape(8, 2, 64, 256), 0).reshape(128, 256)
     gram = lax.all_to_all(gram, "row", 0, 0, axis_index_groups=far, tiled=True)
     gram = jnp.sum(gram.reshape(4, 32, 256), 0)
     return sketch, gram

time: 142 us -> 139 us (0.979)
  waiting for transfers between devices: 29.4 us -> 25.1 us
    ppermute x3, waiting for transfers between devices: 6.25 us -> 3.02 us  [around_ring(): return lax.ppermute(x, ('row', 'col'), pairs)]
  transfers between devices with their start and end apart: 6 -> 6, of which waited for: 4 -> 2; matrix products, arithmetic and copies ran while one was open for 0% -> 0% of each run, Pallas kernels for 1% -> 1%
where the time goes in v9:
time: 139 us; the launch traced here: 138 us
  blocking collectives  84.7 us (61%)
  waiting for transfers between devices  25.1 us (18%)
  starting transfers between devices  17.8 us (13%)
  Pallas kernels  6.84 us (5%)
  local copies, waits for them, and re-layouts  2.6 us (2%)
    all_to_all x1, blocking collectives, shards(): lax.all_to_all(chunks.reshape(GROUPS, TILES, 2, 128), 'row', 0, 0, tiled=...  53.2 us
    all_to_all x1, waiting for transfers between devices, shards(): lax.all_to_all(picked, 'row', 0, 0, tiled=True).reshape(16 * GROUPS, 128)  22.1 us
    all_to_all x1, blocking collectives, shards(): lax.all_to_all(gram, ('row', 'col'), 0, 0, axis_index_groups=near, tiled=...  19.7 us
    all_to_all x1, blocking collectives, shards(): gram = lax.all_to_all(gram, 'row', 0, 0, axis_index_groups=far, tiled=True)  11.8 us
    ppermute x3, starting transfers between devices, around_ring(): return lax.ppermute(x, ('row', 'col'), pairs)  7.76 us
    all_to_all x1, starting transfers between devices, shards(): lax.all_to_all(picked, 'row', 0, 0, tiled=True).reshape(16 * GROUPS, 128)  5.7 us
    ppermute x2, starting transfers between devices, from_partner(): lax.ppermute(x, axis, [(i, i ^ distance) for i in range(lax.axis_size(axi...  4.31 us
    pallas_call x1, Pallas kernels, shards(): call(mix_kernel, shape(16 * GROUPS, 128), [pltpu.VMEM((8 * GROUPS, 128),...  3.67 us
  transfers between devices with their start and end apart: 6, of which 2 were waited for; matrix products, arithmetic and copies ran while one was open for 0% of the time, Pallas kernels for 1%

profile of v9, /device:TPU:8, one launch (start us, length us, event | category | flops | bytes accessed | tf_op | source)
XLA Modules:
  0.0 138.5 jit_solution(11308664882051398421)
XLA Ops:
  0.6 1.2 copy-done
  1.9 0.7 copy-done.3
  2.5 0.7 copy-done.4
  3.2 0.7 shard_map.68
  3.9 0.0 copy-start.1
  4.0 53.2 %all_to_all.28 = f32[64,17,2,128]{3,2,1,0:T(2,128)S(1)} all-to-all(f32[64,17,2,128]{3,2,1,0:T(2,128)S(1)} %bitcast.15), channel_id=1, replica_groups=mesh['row'=64,'col'=8] {'row'}, dimensions={0} | all-to-all | bytes 2228224 | tf_op jit(solution)/shard_map/all_to_all | solution.py:196
  57.1 3.7 %shard_map.69 = f32[1024,128]{1,0:T(8,128)} custom-call(f32[1088,2,128]{2,1,0:T(2,128)S(1)} %bitcast.14, bf16[256,256]{1,0:T(8,128)(2,1)S(1)} %copy-done.2, bf16[512,512]{1,0:T(8,128)(2,1)S(1)} %copy-done.1), custom_call_target="tpu_custom_call" | custom-call | tf_op jit(solution)/shard_map/pallas_call | solution.py:199
  60.8 5.7 %all-to-all-start.1 = ((f32[64,16,128]{2,1,0:T(8,128)}), f32[64,16,128]{2,1,0:T(8,128)S(1)}, u32[]{:S(2)}, u32[]{:S(2)}) async-start(f32[64,16,128]{2,1,0:T(8,128)} %bitcast.5), calls=%async_computation.1 | async-start | bytes 1048576 | tf_op jit(solution)/shard_map/all_to_all | solution.py:203
  66.5 22.1 %all-to-all-done.1 = f32[64,16,128]{2,1,0:T(8,128)S(1)} async-done(((f32[64,16,128]{2,1,0:T(8,128)}), f32[64,16,128]{2,1,0:T(8,128)S(1)}, u32[]{:S(2)}, u32[]{:S(2)}) %all-to-all-start.1) | async-done | bytes 524320 | tf_op jit(solution)/shard_map/all_to_all | solution.py:203
  88.6 0.1 shard_map.70.after_ref
  88.7 1.9 %collective-permute-start = (f32[128,512]{1,0:T(8,128)S(1)}, f32[128,512]{1,0:T(8,128)S(1)}, u32[]{:S(2)}, u32[]{:S(2)}) collective-permute-start(f32[128,512]{1,0:T(8,128)S(1)} %shard_map.70.after_ref), channel_id=1, source_target_pairs={{0,4},{1,13},{2,6},{3,15},{4,8},{5,1},{6,10},{7,3},{8,12},{9,5},{1... | collective-permute-start | bytes 786440 | tf_op jit(solution)/shard_map/ppermute | solution.py:189
  90.6 0.3 shard_map.71
  90.9 2.0 %collective-permute-start.1 = (f32[128,512]{1,0:T(8,128)S(1)}, f32[128,512]{1,0:T(8,128)S(1)}, u32[]{:S(2)}, u32[]{:S(2)}) collective-permute-start(f32[128,512]{1,0:T(8,128)S(1)} %get-tuple-element.10), channel_id=1, source_target_pairs={{0,2},{1,3},{2,4},{3,5},{4,6},{5,7},{6,8},{7,9},{8,10},{9,11},{10,... | collective-permute-start | bytes 786440 | tf_op jit(solution)/shard_map/ppermute | solution.py:189
  92.9 3.8 %collective-permute-start.2 = (f32[128,512]{1,0:T(8,128)S(1)}, f32[128,512]{1,0:T(8,128)S(1)}, u32[]{:S(2)}, u32[]{:S(2)}) collective-permute-start(f32[128,512]{1,0:T(8,128)S(1)} %get-tuple-element.11), channel_id=1, source_target_pairs={{0,14},{1,15},{2,0},{3,1},{4,2},{5,3},{6,4},{7,5},{8,6},{9,7},{10,... | collective-permute-start | bytes 786440 | tf_op jit(solution)/shard_map/ppermute | solution.py:189
  96.8 0.9 shard_map.72
  97.6 1.9 %collective-permute-start.3 = (f32[256,256]{1,0:T(8,128)S(1)}, f32[256,256]{1,0:T(8,128)S(1)}, u32[]{:S(2)}, u32[]{:S(2)}) collective-permute-start(f32[256,256]{1,0:T(8,128)S(1)} %get-tuple-element.12.right_ref), channel_id=1, source_target_pairs={{0,1},{1,0},{2,3},{3,2},{4,5},{5,4},{6,7},{7,6},{8,9},{9,8},{10,11... | collective-permute-start | bytes 786440 | tf_op jit(solution)/shard_map/ppermute | solution.py:181
  99.5 2.4 %collective-permute-start.4 = (f32[256,256]{1,0:T(8,128)S(1)}, f32[256,256]{1,0:T(8,128)S(1)}, u32[]{:S(2)}, u32[]{:S(2)}) collective-permute-start(f32[256,256]{1,0:T(8,128)S(1)} %get-tuple-element.13.right_too_ref), channel_id=1, source_target_pairs={{0,1},{1,0},{2,3},{3,2},{4,5},{5,4},{6,7},{7,6},{8,9},{9,8},{10,11... | collective-permute-start | bytes 786440 | tf_op jit(solution)/shard_map/ppermute | solution.py:181
  101.9 3.0 %collective-permute-done.1.up_ref = f32[128,512]{1,0:T(8,128)S(1)} collective-permute-done((f32[128,512]{1,0:T(8,128)S(1)}, f32[128,512]{1,0:T(8,128)S(1)}, u32[]{:S(2)}, u32[]{:S(2)}) %collective-permute-start.1) | collective-permute-done | bytes 262176 | tf_op jit(solution)/shard_map/ppermute | solution.py:189
  105.0 0.6 shard_map.73.half_ref
  105.6 0.7 shard_map.74
  106.3 19.7 %all_to_all.29 = f32[16,64,256]{2,1,0:T(8,128)S(1)} all-to-all(f32[16,64,256]{2,1,0:T(8,128)S(1)} %bitcast.16), channel_id=1, replica_groups={{0,1,16,17,128,129,144,145,256,257,272,273,384,385,400,401},{2,3,18,19,..., dimensions={0} | all-to-all | bytes 2097152 | tf_op jit(solution)/shard_map/all_to_all | solution.py:237
  126.0 0.1 reduce_sum.18
  126.1 11.8 %all_to_all.30 = f32[4,32,256]{2,1,0:T(8,128)S(1)} all-to-all(f32[4,32,256]{2,1,0:T(8,128)S(1)} %bitcast.20), channel_id=1, replica_groups={{0,32,64,96},{8,40,72,104},{16,48,80,112},{24,56,88,120},{128,160,192,2..., dimensions={0} | all-to-all | bytes 262144 | tf_op jit(solution)/shard_map/all_to_all | solution.py:239
  137.9 0.6 reduce_sum.19
  (10 shorter events, 0.0 us)
Async XLA Ops:
  0.6 1.2 copy-start
  1.9 0.7 copy-start.3
  2.5 0.7 copy-start.4
  3.9 53.2 %copy-start.1 = (bf16[512,512]{1,0:T(8,128)(2,1)S(1)}, bf16[512,512]{1,0:T(8,128)(2,1)}, u32[]{:S(2)}) copy-start(bf16[512,512]{1,0:T(8,128)(2,1)} %constant.18.clone.lane_table_ref) | copy-start | bytes 1572868
  3.9 53.2 %copy-start.2 = (bf16[256,256]{1,0:T(8,128)(2,1)S(1)}, bf16[256,256]{1,0:T(8,128)(2,1)}, u32[]{:S(2)}) copy-start(bf16[256,256]{1,0:T(8,128)(2,1)} %constant.17.clone.block_table_ref) | copy-start | bytes 393220
  60.8 27.8 %all-to-all-start.1 = ((f32[64,16,128]{2,1,0:T(8,128)}), f32[64,16,128]{2,1,0:T(8,128)S(1)}, u32[]{:S(2)}, u32[]{:S(2)}) async-start(f32[64,16,128]{2,1,0:T(8,128)} %bitcast.5), calls=%async_computation.1 | async-start | bytes 1048576 | tf_op jit(solution)/shard_map/all_to_all | solution.py:203
  88.7 13.2 %collective-permute-start = (f32[128,512]{1,0:T(8,128)S(1)}, f32[128,512]{1,0:T(8,128)S(1)}, u32[]{:S(2)}, u32[]{:S(2)}) collective-permute-start(f32[128,512]{1,0:T(8,128)S(1)} %shard_map.70.after_ref), channel_id=1, source_target_pairs={{0,4},{1,13},{2,6},{3,15},{4,8},{5,1},{6,10},{7,3},{8,12},{9,5},{1... | collective-permute-start | bytes 786440 | tf_op jit(solution)/shard_map/ppermute | solution.py:189
  90.9 14.1 %collective-permute-start.1 = (f32[128,512]{1,0:T(8,128)S(1)}, f32[128,512]{1,0:T(8,128)S(1)}, u32[]{:S(2)}, u32[]{:S(2)}) collective-permute-start(f32[128,512]{1,0:T(8,128)S(1)} %get-tuple-element.10), channel_id=1, source_target_pairs={{0,2},{1,3},{2,4},{3,5},{4,6},{5,7},{6,8},{7,9},{8,10},{9,11},{10,... | collective-permute-start | bytes 786440 | tf_op jit(solution)/shard_map/ppermute | solution.py:189
  92.9 12.1 %collective-permute-start.2 = (f32[128,512]{1,0:T(8,128)S(1)}, f32[128,512]{1,0:T(8,128)S(1)}, u32[]{:S(2)}, u32[]{:S(2)}) collective-permute-start(f32[128,512]{1,0:T(8,128)S(1)} %get-tuple-element.11), channel_id=1, source_target_pairs={{0,14},{1,15},{2,0},{3,1},{4,2},{5,3},{6,4},{7,5},{8,6},{9,7},{10,... | collective-permute-start | bytes 786440 | tf_op jit(solution)/shard_map/ppermute | solution.py:189
  97.6 8.0 %collective-permute-start.3 = (f32[256,256]{1,0:T(8,128)S(1)}, f32[256,256]{1,0:T(8,128)S(1)}, u32[]{:S(2)}, u32[]{:S(2)}) collective-permute-start(f32[256,256]{1,0:T(8,128)S(1)} %get-tuple-element.12.right_ref), channel_id=1, source_target_pairs={{0,1},{1,0},{2,3},{3,2},{4,5},{5,4},{6,7},{7,6},{8,9},{9,8},{10,11... | collective-permute-start | bytes 786440 | tf_op jit(solution)/shard_map/ppermute | solution.py:181
  99.5 6.1 %collective-permute-start.4 = (f32[256,256]{1,0:T(8,128)S(1)}, f32[256,256]{1,0:T(8,128)S(1)}, u32[]{:S(2)}, u32[]{:S(2)}) collective-permute-start(f32[256,256]{1,0:T(8,128)S(1)} %get-tuple-element.13.right_too_ref), channel_id=1, source_target_pairs={{0,1},{1,0},{2,3},{3,2},{4,5},{5,4},{6,7},{7,6},{8,9},{9,8},{10,11... | collective-permute-start | bytes 786440 | tf_op jit(solution)/shard_map/ppermute | solution.py:181

commit v10 on v9

--- a/solution.py
+++ b/solution.py
@@ -50,30 +50,25 @@
         )
 
 
-def mix_kernel(chunks_ref, block_table_ref, lane_table_ref, out_ref, *mixed):
+def mix_kernel(chunks_ref, block_table_ref, lane_table_ref, out_ref, mixed):
+    columns = []
+    for v in range(4):
+        rows = [
+            chunks_ref[pl.ds(v * 4 + q, GROUPS, stride=TILES), half, :] for q in range(4) for half in range(2)
+        ]
+        columns.append(jnp.concatenate(rows, 0))
+    high, low = split(jnp.concatenate(columns, 1))
     block_table = block_table_ref[...]
+    high, low = split(dot(block_table, high) + dot(block_table, low))
     lane_table = lane_table_ref[...]
-    for pair in range(2):
-        columns = []
-        for v in range(4):
-            rows = [
-                chunks_ref[pl.ds(v * 4 + q, GROUPS, stride=TILES), half, :]
-                for q in (2 * pair, 2 * pair + 1)
-                for half in range(2)
-            ]
-            columns.append(jnp.concatenate(rows, 0))
-        high, low = split(jnp.concatenate(columns, 1))
-        high, low = split(dot(block_table, high) + dot(block_table, low))
-        done = (dot(high, lane_table) + dot(low, lane_table)) * F32(2.0**-8)
-        for v in range(4):
-            mixed[v][pair * 256 : pair * 256 + 256, :] = done[:, v * 128 : v * 128 + 128]
+    mixed[...] = (dot(high, lane_table) + dot(low, lane_table)) * F32(2.0**-8)
     even = jnp.bitwise_and(lax.broadcasted_iota(jnp.int32, (8, 128), 0), 1) == 0
 
     def eight(group, carry):
         for inner in range(8):
             block = group * 8 + inner
             local_picks = chunks_ref[block * TILES + 16].astype(jnp.int32)
-            sources = [mixed[v][pl.ds(block, 8, stride=GROUPS), :] for v in range(4)]
+            sources = [mixed[block * 8 : block * 8 + 8, v * 128 : v * 128 + 128] for v in range(4)]
             found = []
             for part in range(2):
                 local = jnp.broadcast_to(local_picks[part : part + 1, :], (8, 128))
@@ -194,9 +189,10 @@
         matrix, signs[None, :], picks.reshape(2, 128)
     )
     chunks = lax.all_to_all(chunks.reshape(GROUPS, TILES, 2, 128), "row", 0, 0, tiled=True)
-    block_table = jnp.asarray(np.kron(np.eye(2), sylvester(2 * GROUPS)), BF16)
+    block_table = np.kron(np.eye(4), sylvester(2 * GROUPS)).reshape(8, GROUPS, 8 * GROUPS)
+    block_table = jnp.asarray(block_table.transpose(1, 0, 2).reshape(8 * GROUPS, 8 * GROUPS), BF16)
     lane_table = jnp.asarray(sylvester(LANES), BF16)
-    picked = call(mix_kernel, shape(16 * GROUPS, 128), [pltpu.VMEM((8 * GROUPS, 128), F32)] * 4)(
+    picked = call(mix_kernel, shape(16 * GROUPS, 128), [pltpu.VMEM((8 * GROUPS, LANES), F32)])(
         chunks.reshape(GROUPS * TILES, 2, 128), block_table, lane_table
     )
     picked = picked.reshape(GROUPS, 16, 128)

time: 139 us -> 139 us (level)
  no operation moved by 1% of the time
where the time goes in v10:
time: 139 us; the launch traced here: 138 us
  blocking collectives  84.7 us (61%)
  waiting for transfers between devices  25.1 us (18%)
  starting transfers between devices  17.8 us (13%)
  Pallas kernels  6.81 us (5%)
  local copies, waits for them, and re-layouts  2.6 us (2%)
    all_to_all x1, blocking collectives, shards(): lax.all_to_all(chunks.reshape(GROUPS, TILES, 2, 128), 'row', 0, 0, tiled=...  53.2 us
    all_to_all x1, waiting for transfers between devices, shards(): lax.all_to_all(picked, 'row', 0, 0, tiled=True).reshape(16 * GROUPS, 128)  22.1 us
    all_to_all x1, blocking collectives, shards(): lax.all_to_all(gram, ('row', 'col'), 0, 0, axis_index_groups=near, tiled=...  19.7 us
    all_to_all x1, blocking collectives, shards(): gram = lax.all_to_all(gram, 'row', 0, 0, axis_index_groups=far, tiled=True)  11.8 us
    ppermute x3, starting transfers between devices, around_ring(): return lax.ppermute(x, ('row', 'col'), pairs)  7.76 us
    all_to_all x1, starting transfers between devices, shards(): lax.all_to_all(picked, 'row', 0, 0, tiled=True).reshape(16 * GROUPS, 128)  5.7 us
    ppermute x2, starting transfers between devices, from_partner(): lax.ppermute(x, axis, [(i, i ^ distance) for i in range(lax.axis_size(axi...  4.31 us
    pallas_call x1, Pallas kernels, shards(): call(mix_kernel, shape(16 * GROUPS, 128), [pltpu.VMEM((8 * GROUPS, LANES)...  3.63 us
  transfers between devices with their start and end apart: 6, of which 2 were waited for; matrix products, arithmetic and copies ran while one was open for 0% of the time, Pallas kernels for 1%

profile of v10, /device:TPU:8, one launch (start us, length us, event | category | flops | bytes accessed | tf_op | source)
XLA Modules:
  0.0 138.5 jit_solution(34072287425234764)
XLA Ops:
  0.6 1.2 copy-done
  1.9 0.7 copy-done.3
  2.5 0.7 copy-done.4
  3.2 0.7 shard_map.68
  3.9 0.0 copy-start.1
  4.0 53.2 %all_to_all.28 = f32[64,17,2,128]{3,2,1,0:T(2,128)S(1)} all-to-all(f32[64,17,2,128]{3,2,1,0:T(2,128)S(1)} %bitcast.15), channel_id=1, replica_groups=mesh['row'=64,'col'=8] {'row'}, dimensions={0} | all-to-all | bytes 2228224 | tf_op jit(solution)/shard_map/all_to_all | solution.py:191
  57.1 3.6 %shard_map.69 = f32[1024,128]{1,0:T(8,128)} custom-call(f32[1088,2,128]{2,1,0:T(2,128)S(1)} %bitcast.14, bf16[512,512]{1,0:T(8,128)(2,1)S(1)} %copy-done.2, bf16[512,512]{1,0:T(8,128)(2,1)S(1)} %copy-done.1), custom_call_target="tpu_custom_call" | custom-call | tf_op jit(solution)/shard_map/pallas_call | solution.py:195
  60.8 5.7 %all-to-all-start.1 = ((f32[64,16,128]{2,1,0:T(8,128)}), f32[64,16,128]{2,1,0:T(8,128)S(1)}, u32[]{:S(2)}, u32[]{:S(2)}) async-start(f32[64,16,128]{2,1,0:T(8,128)} %bitcast.5), calls=%async_computation.1 | async-start | bytes 1048576 | tf_op jit(solution)/shard_map/all_to_all | solution.py:199
  66.5 22.1 %all-to-all-done.1 = f32[64,16,128]{2,1,0:T(8,128)S(1)} async-done(((f32[64,16,128]{2,1,0:T(8,128)}), f32[64,16,128]{2,1,0:T(8,128)S(1)}, u32[]{:S(2)}, u32[]{:S(2)}) %all-to-all-start.1) | async-done | bytes 524320 | tf_op jit(solution)/shard_map/all_to_all | solution.py:199
  88.6 0.1 shard_map.70.after_ref
  88.7 1.9 %collective-permute-start = (f32[128,512]{1,0:T(8,128)S(1)}, f32[128,512]{1,0:T(8,128)S(1)}, u32[]{:S(2)}, u32[]{:S(2)}) collective-permute-start(f32[128,512]{1,0:T(8,128)S(1)} %shard_map.70.after_ref), channel_id=1, source_target_pairs={{0,4},{1,13},{2,6},{3,15},{4,8},{5,1},{6,10},{7,3},{8,12},{9,5},{1... | collective-permute-start | bytes 786440 | tf_op jit(solution)/shard_map/ppermute | solution.py:184
  90.6 0.3 shard_map.71
  90.9 2.0 %collective-permute-start.1 = (f32[128,512]{1,0:T(8,128)S(1)}, f32[128,512]{1,0:T(8,128)S(1)}, u32[]{:S(2)}, u32[]{:S(2)}) collective-permute-start(f32[128,512]{1,0:T(8,128)S(1)} %get-tuple-element.10), channel_id=1, source_target_pairs={{0,2},{1,3},{2,4},{3,5},{4,6},{5,7},{6,8},{7,9},{8,10},{9,11},{10,... | collective-permute-start | bytes 786440 | tf_op jit(solution)/shard_map/ppermute | solution.py:184
  92.9 3.8 %collective-permute-start.2 = (f32[128,512]{1,0:T(8,128)S(1)}, f32[128,512]{1,0:T(8,128)S(1)}, u32[]{:S(2)}, u32[]{:S(2)}) collective-permute-start(f32[128,512]{1,0:T(8,128)S(1)} %get-tuple-element.11), channel_id=1, source_target_pairs={{0,14},{1,15},{2,0},{3,1},{4,2},{5,3},{6,4},{7,5},{8,6},{9,7},{10,... | collective-permute-start | bytes 786440 | tf_op jit(solution)/shard_map/ppermute | solution.py:184
  96.7 0.9 shard_map.72
  97.6 1.9 %collective-permute-start.3 = (f32[256,256]{1,0:T(8,128)S(1)}, f32[256,256]{1,0:T(8,128)S(1)}, u32[]{:S(2)}, u32[]{:S(2)}) collective-permute-start(f32[256,256]{1,0:T(8,128)S(1)} %get-tuple-element.12.right_ref), channel_id=1, source_target_pairs={{0,1},{1,0},{2,3},{3,2},{4,5},{5,4},{6,7},{7,6},{8,9},{9,8},{10,11... | collective-permute-start | bytes 786440 | tf_op jit(solution)/shard_map/ppermute | solution.py:176
  99.5 2.4 %collective-permute-start.4 = (f32[256,256]{1,0:T(8,128)S(1)}, f32[256,256]{1,0:T(8,128)S(1)}, u32[]{:S(2)}, u32[]{:S(2)}) collective-permute-start(f32[256,256]{1,0:T(8,128)S(1)} %get-tuple-element.13.right_too_ref), channel_id=1, source_target_pairs={{0,1},{1,0},{2,3},{3,2},{4,5},{5,4},{6,7},{7,6},{8,9},{9,8},{10,11... | collective-permute-start | bytes 786440 | tf_op jit(solution)/shard_map/ppermute | solution.py:176
  101.9 3.0 %collective-permute-done.1.up_ref = f32[128,512]{1,0:T(8,128)S(1)} collective-permute-done((f32[128,512]{1,0:T(8,128)S(1)}, f32[128,512]{1,0:T(8,128)S(1)}, u32[]{:S(2)}, u32[]{:S(2)}) %collective-permute-start.1) | collective-permute-done | bytes 262176 | tf_op jit(solution)/shard_map/ppermute | solution.py:184
  104.9 0.6 shard_map.73.half_ref
  105.6 0.7 shard_map.74
  106.3 19.7 %all_to_all.29 = f32[16,64,256]{2,1,0:T(8,128)S(1)} all-to-all(f32[16,64,256]{2,1,0:T(8,128)S(1)} %bitcast.16), channel_id=1, replica_groups={{0,1,16,17,128,129,144,145,256,257,272,273,384,385,400,401},{2,3,18,19,..., dimensions={0} | all-to-all | bytes 2097152 | tf_op jit(solution)/shard_map/all_to_all | solution.py:233
  126.0 0.1 reduce_sum.18
  126.0 11.8 %all_to_all.30 = f32[4,32,256]{2,1,0:T(8,128)S(1)} all-to-all(f32[4,32,256]{2,1,0:T(8,128)S(1)} %bitcast.20), channel_id=1, replica_groups={{0,32,64,96},{8,40,72,104},{16,48,80,112},{24,56,88,120},{128,160,192,2..., dimensions={0} | all-to-all | bytes 262144 | tf_op jit(solution)/shard_map/all_to_all | solution.py:235
  137.8 0.6 reduce_sum.19
  (10 shorter events, 0.0 us)
Async XLA Ops:
  0.6 1.2 copy-start
  1.9 0.7 copy-start.3
  2.5 0.7 copy-start.4
  3.9 53.2 %copy-start.1 = (bf16[512,512]{1,0:T(8,128)(2,1)S(1)}, bf16[512,512]{1,0:T(8,128)(2,1)}, u32[]{:S(2)}) copy-start(bf16[512,512]{1,0:T(8,128)(2,1)} %constant.18.clone.lane_table_ref) | copy-start | bytes 1572868
  3.9 53.2 %copy-start.2 = (bf16[512,512]{1,0:T(8,128)(2,1)S(1)}, bf16[512,512]{1,0:T(8,128)(2,1)}, u32[]{:S(2)}) copy-start(bf16[512,512]{1,0:T(8,128)(2,1)} %constant.17.clone.block_table_ref) | copy-start | bytes 1572868
  60.8 27.8 %all-to-all-start.1 = ((f32[64,16,128]{2,1,0:T(8,128)}), f32[64,16,128]{2,1,0:T(8,128)S(1)}, u32[]{:S(2)}, u32[]{:S(2)}) async-start(f32[64,16,128]{2,1,0:T(8,128)} %bitcast.5), calls=%async_computation.1 | async-start | bytes 1048576 | tf_op jit(solution)/shard_map/all_to_all | solution.py:199
  88.7 13.2 %collective-permute-start = (f32[128,512]{1,0:T(8,128)S(1)}, f32[128,512]{1,0:T(8,128)S(1)}, u32[]{:S(2)}, u32[]{:S(2)}) collective-permute-start(f32[128,512]{1,0:T(8,128)S(1)} %shard_map.70.after_ref), channel_id=1, source_target_pairs={{0,4},{1,13},{2,6},{3,15},{4,8},{5,1},{6,10},{7,3},{8,12},{9,5},{1... | collective-permute-start | bytes 786440 | tf_op jit(solution)/shard_map/ppermute | solution.py:184
  90.9 14.1 %collective-permute-start.1 = (f32[128,512]{1,0:T(8,128)S(1)}, f32[128,512]{1,0:T(8,128)S(1)}, u32[]{:S(2)}, u32[]{:S(2)}) collective-permute-start(f32[128,512]{1,0:T(8,128)S(1)} %get-tuple-element.10), channel_id=1, source_target_pairs={{0,2},{1,3},{2,4},{3,5},{4,6},{5,7},{6,8},{7,9},{8,10},{9,11},{10,... | collective-permute-start | bytes 786440 | tf_op jit(solution)/shard_map/ppermute | solution.py:184
  92.9 12.1 %collective-permute-start.2 = (f32[128,512]{1,0:T(8,128)S(1)}, f32[128,512]{1,0:T(8,128)S(1)}, u32[]{:S(2)}, u32[]{:S(2)}) collective-permute-start(f32[128,512]{1,0:T(8,128)S(1)} %get-tuple-element.11), channel_id=1, source_target_pairs={{0,14},{1,15},{2,0},{3,1},{4,2},{5,3},{6,4},{7,5},{8,6},{9,7},{10,... | collective-permute-start | bytes 786440 | tf_op jit(solution)/shard_map/ppermute | solution.py:184
  97.6 8.0 %collective-permute-start.3 = (f32[256,256]{1,0:T(8,128)S(1)}, f32[256,256]{1,0:T(8,128)S(1)}, u32[]{:S(2)}, u32[]{:S(2)}) collective-permute-start(f32[256,256]{1,0:T(8,128)S(1)} %get-tuple-element.12.right_ref), channel_id=1, source_target_pairs={{0,1},{1,0},{2,3},{3,2},{4,5},{5,4},{6,7},{7,6},{8,9},{9,8},{10,11... | collective-permute-start | bytes 786440 | tf_op jit(solution)/shard_map/ppermute | solution.py:176
  99.5 6.1 %collective-permute-start.4 = (f32[256,256]{1,0:T(8,128)S(1)}, f32[256,256]{1,0:T(8,128)S(1)}, u32[]{:S(2)}, u32[]{:S(2)}) collective-permute-start(f32[256,256]{1,0:T(8,128)S(1)} %get-tuple-element.13.right_too_ref), channel_id=1, source_target_pairs={{0,1},{1,0},{2,3},{3,2},{4,5},{5,4},{6,7},{7,6},{8,9},{9,8},{10,11... | collective-permute-start | bytes 786440 | tf_op jit(solution)/shard_map/ppermute | solution.py:176
